TPU v7x, 32 devices: a whole 2x2x4 slice. The times are simulated.
32 devices in a mesh: gx: 2 (over y), gy: 4 (over x, core), gz: 4 (over z).
Axes of the slice: x: 2, y: 2, z: 4, core: 2. Of those that a mesh axis runs over, the one named last changes fastest.
Arguments:
- offsets: float32 [3, 4, 8, 8, 128], P(None, 'gx', 'gy', 'gz'), may hold values from -0.5 to 0.5
- lines: float32 [3, 4, 8, 8, 128], P(None, 'gx', 'gy', 'gz'), may hold values from -4 to 4
- burgers: float32 [3, 4, 8, 8, 128], P(None, 'gx', 'gy', 'gz'), may hold values from -4 to 4
- counts: int32 [4, 8, 8], P('gx', 'gy', 'gz'), may hold values from 64 to 128, as said below
- mobility: float32 [4, 8, 8], P('gx', 'gy', 'gz'), may hold values from 0.5 to 2
- stress: float32 [3, 3], replicated, may hold values from -3 to 3
- translation: float32 [128, 128], replicated, may hold values from -0.625 to 0.625
Outputs:
- velocity: float32 [3, 4, 8, 8, 128], P(None, 'gx', 'gy', 'gz')
Inputs may be any that keep to these rules, and one draw needn't show every extreme that they name: `counts`: some cell holds 128 live segments.
All inputs are finite; a program needn't handle non-finite values.
Results may differ from a plain program's by a relative error of at most 0.0003.
Values sent between devices are 32-bit elements; how exact they have to be, the bound alone decides.
No kernel may reach another device: no remote copies, remote signals or barrier semaphores. Data moves between devices by JAX's collectives and lax.ppermute only.
A program may use at most 64 MiB of HBM per device.

v0:
```python
import jax
import jax.numpy as jnp
from jax import lax
from jax.sharding import PartitionSpec as P

core_square = 0.0625
near_scale = 0.01
highest = lax.Precision.HIGHEST


def padded_2(value, sides, width):
    for axis, dim in sides:
        count, length = (lax.axis_size(axis), value.shape[dim])
        up = [(i, (i + 1) % count) for i in range(count)]
        down = [(j, i) for i, j in up]
        last = lax.slice_in_dim(value, length - width, length, axis=dim)
        first = lax.slice_in_dim(value, 0, width, axis=dim)
        before = lax.ppermute(last, axis, up)
        after = lax.ppermute(first, axis, down)
        value = jnp.concatenate([before, value, after], axis=dim)
    return value


def exponent_list():
    result = []
    for first in range(5):
        for second in range(5 - first):
            for third in range(5 - first - second):
                result.append((first, second, third))
    return result


def monomials(relative):
    powers = []
    for column in range(3):
        base = relative[column]
        square = base * base
        powers.append([jnp.ones_like(base), base, square, square * base, square * square])
    return jnp.stack(
        [
            powers[0][first] * powers[1][second] * powers[2][third]
            for first, second, third in exponent_list()
        ]
    )


def crossed(left, right):
    return jnp.stack(
        [
            left[1] * right[2] - left[2] * right[1],
            left[2] * right[0] - left[0] * right[2],
            left[0] * right[1] - left[1] * right[0],
        ]
    )


def pair_forces(target, source, shift):
    separation = [
        shift[column] + source[column][..., None, :] - target[column][..., :, None]
        for column in range(3)
    ]
    radius_sq = (
        separation[0] * separation[0]
        + separation[1] * separation[1]
        + separation[2] * separation[2]
        + core_square
    )
    inverse = 1.0 / (radius_sq * jnp.sqrt(radius_sq))
    burgers_dot = sum(
        (target[6 + column][..., :, None] * source[6 + column][..., None, :] for column in range(3))
    )
    line_dot = sum(
        (target[3 + column][..., :, None] * source[3 + column][..., None, :] for column in range(3))
    )
    target_proj = sum(
        (target[6 + column][..., :, None] * separation[column] for column in range(3))
    )
    source_proj = sum(
        (source[6 + column][..., None, :] * separation[column] for column in range(3))
    )
    first_coef = inverse * burgers_dot * line_dot
    second_coef = inverse * target_proj * source_proj / radius_sq
    return jnp.stack(
        [
            jnp.sum(
                first_coef * separation[column] + second_coef * source[3 + column][..., None, :], -1
            )
            for column in range(3)
        ]
    )


def near_total(inner, padded):
    extent = inner.shape[1:4]
    total = jnp.zeros((3,) + inner.shape[1:], jnp.float32)
    for step_x in (-1, 0, 1):
        for step_y in (-1, 0, 1):
            for step_z in (-1, 0, 1):
                source = padded[
                    :,
                    1 + step_x : 1 + step_x + extent[0],
                    1 + step_y : 1 + step_y + extent[1],
                    1 + step_z : 1 + step_z + extent[2],
                ]
                total = total + pair_forces(
                    inner, source, (float(step_x), float(step_y), float(step_z))
                )
    return near_scale * total


def cell_moments(poly, charge, slots, width):
    moments = jnp.einsum("kxyzs,cxyzs->xyzck", poly, charge, precision=highest) / slots
    flat = moments.reshape(-1, 3 * poly.shape[0])
    return jnp.pad(flat, ((0, 0), (0, width - flat.shape[1])))


def far_weights(rows_first, rows_second, extents):
    total_sq = jnp.zeros((rows_first[0].shape[0], rows_second[0].shape[0]), jnp.float32)
    largest = jnp.zeros((rows_first[0].shape[0], rows_second[0].shape[0]), jnp.int32)
    for column in range(3):
        spacing = (
            jnp.abs(rows_first[column][:, None] - rows_second[column][None, :]) % extents[column]
        )
        spacing = jnp.minimum(spacing, extents[column] - spacing)
        largest = jnp.maximum(largest, spacing)
        total_sq = total_sq + spacing.astype(jnp.float32) * spacing.astype(jnp.float32)
    return jnp.where(largest > 1, 1.0 / jnp.sqrt(jnp.maximum(total_sq, 1.0)), 0.0)


def finish(lines, charge, mask, poly, near, coefficients, mobility, stress):
    terms = poly.shape[0]
    blocks = coefficients[..., : 3 * terms].reshape(coefficients.shape[:3] + (3, terms))
    far = jnp.einsum("kxyzs,xyzak->axyzs", poly, blocks, precision=highest)
    stressed = jnp.stack(
        [sum((stress[row, column] * charge[column] for column in range(3))) for row in range(3)]
    )
    applied = crossed(stressed, lines)
    force = near + far * mask + applied
    along = jnp.sum(force * lines, 0) / jnp.maximum(jnp.sum(lines * lines, 0), 1.0)
    return mobility[..., None] * mask * (force - along * lines)


def body(offsets, lines, burgers, counts, mobility, stress, translation):
    slots = offsets.shape[-1]
    edge = offsets.shape[1:4]
    mask = (lax.broadcasted_iota(jnp.int32, counts.shape + (slots,), 3) < counts[..., None]).astype(
        jnp.float32
    )
    charge = burgers * mask
    stacked = jnp.concatenate([offsets, lines, charge], 0)
    padded = padded_2(stacked, (("gx", 1), ("gy", 2), ("gz", 3)), 1)
    poly = monomials(offsets)
    moments = cell_moments(poly, crossed(charge, lines), slots, translation.shape[0])
    devices_along = (lax.axis_size("gx"), lax.axis_size("gy"), lax.axis_size("gz"))
    extents = (edge[0] * devices_along[0], edge[1] * devices_along[1], edge[2] * devices_along[2])
    local_cells = edge[0] * edge[1] * edge[2]
    local_index = jnp.arange(local_cells, dtype=jnp.int32)
    mine = (
        lax.axis_index("gx") * edge[0] + local_index // (edge[1] * edge[2]),
        lax.axis_index("gy") * edge[1] + local_index // edge[2] % edge[1],
        lax.axis_index("gz") * edge[2] + local_index % edge[2],
    )
    piece = lax.all_gather(moments, ("gx", "gy", "gz"), axis=0, tiled=True)
    rows = jnp.arange(piece.shape[0], dtype=jnp.int32)
    device = rows // local_cells
    within = rows % local_cells
    weights = far_weights(
        mine,
        (
            device // (devices_along[1] * devices_along[2]) * edge[0]
            + within // (edge[1] * edge[2]),
            device // devices_along[2] % devices_along[1] * edge[1] + within // edge[2] % edge[1],
            device % devices_along[2] * edge[2] + within % edge[2],
        ),
        extents,
    )
    local = jnp.dot(weights, piece, precision=highest, preferred_element_type=jnp.float32)
    near = near_total(stacked, padded)
    coefficients = jnp.dot(
        local, translation, precision=highest, preferred_element_type=jnp.float32
    )
    coefficients = coefficients.reshape(edge[0], edge[1], edge[2], -1)
    return finish(lines, charge, mask, poly, near, coefficients, mobility, stress)


def solution(mesh):
    placed = (
        P(None, "gx", "gy", "gz", None),
        P(None, "gx", "gy", "gz", None),
        P(None, "gx", "gy", "gz", None),
        P("gx", "gy", "gz"),
        P("gx", "gy", "gz"),
        P(),
        P(),
    )
    return jax.shard_map(
        body, mesh=mesh, in_specs=placed, out_specs=P(None, "gx", "gy", "gz", None), check_vma=False
    )
```

profile of v0, /device:TPU:0, one launch (start us, length us, event | category | flops | bytes accessed | tf_op | source)
XLA Modules:
  0.0 150.3 jit_solution(18174777846973374702)
XLA Ops:
  1.6 3.0 %collective-permute-start = (f32[9,1,2,2,128]{4,3,2,1,0:T(2,128)S(1)}, f32[9,1,2,2,128]{4,3,2,1,0:T(2,128)S(1)}, u32[]{:S(2)}, u32[]{:S(2)}) collective-permute-start(f32[9,1,2,2,128]{4,3,2,1,0:T(2,128)S(1)} %get-tuple-element.336), channel_id=1, source_target_pairs={{0,16},{16,0},{1,17},{17,1},{2,18},{18,2},{3,19},{19,3},{4,20},{20... | collective-permute-start | bytes 55304 | tf_op jit(solution)/shard_map/ppermute | solution.py:18
  7.0 3.7 %multiply_subtract_fusion.2 = (f32[1,2,2,2,128]{4,3,2,1,0:T(2,128)S(1)}, f32[1,2,2,2,128]{4,3,2,1,0:T(2,128)S(1)}, f32[1,2,2,2,128]{4,3,2,1,0:T(2,128)S(1)}, f32...) fusion(f32[3,2,2,2,128]{4,3,2,1,0:T(2,128)S(1)} %copy-done.2, ...), kind=kLoop, calls=%fused_computation.1256 | loop fusion | flops 16384 | bytes 53272 | tf_op jit(solution)/shard_map/sub | solution.py:50
  15.4 68.8 %all_gather.3 = f32[256,128]{1,0:T(8,128)S(1)} all-gather(f32[8,128]{1,0:T(8,128)S(1)} %pad.4), channel_id=1, replica_groups=mesh['gx'=2,'gy'=4,'gz'=4] {'gx','gy','gz'}, dimensions={0}, use_global_device_ids=true | all-gather | bytes 135168 | tf_op jit(solution)/shard_map/all_gather | solution.py:163
  86.9 2.2 %fusion.95 = (f32[2,2,2,128]{3,2,1,0:T(2,128)S(1)}, f32[2,2,2,128]{3,2,1,0:T(2,128)S(1)}, f32[2,2,2,128]{3,2,1,0:T(2,128)S(1)}) fusion(f32[2,2,2,128]{3,2,1,0:T(2,128)S(1)} %get-tuple-element.319, f32[2,2,2,128]{3,2,1,0:T(2,128)S(1)} %get-tuple-element.334, f32[2,2,2,128]{3,2,1,0:T(2,128)S(1)} %get-tuple-element.342, ...), kind=kLoop, calls=%fused_computation.447 | loop fusion | flops 6288384 | bytes 86016 | tf_op jit(solution)/shard_map/reduce_sum | solution.py:85
  89.9 3.8 %collective-permute-start.5 = (f32[9,4,4,1,128]{4,3,2,1,0:T(1,128)S(1)}, f32[9,4,4,1,128]{4,3,2,1,0:T(1,128)S(1)}, u32[]{:S(2)}, u32[]{:S(2)}) collective-permute-start(f32[9,4,4,1,128]{4,3,2,1,0:T(1,128)S(1)} %get-tuple-element.259), channel_id=1, source_target_pairs={{1,0},{2,1},{3,2},{0,3},{5,4},{6,5},{7,6},{4,7},{9,8},{10,9},{11,1... | collective-permute-start | bytes 221192 | tf_op jit(solution)/shard_map/ppermute | solution.py:19
  95.9 2.2 %fusion.47 = (f32[2,2,2,128]{3,2,1,0:T(2,128)S(1)}, f32[2,2,2,128]{3,2,1,0:T(2,128)S(1)}, f32[2,2,2,128]{3,2,1,0:T(2,128)S(1)}) fusion(f32[2,2,2,128]{3,2,1,0:T(2,128)S(1)} %get-tuple-element.380, f32[2,2,2,128]{3,2,1,0:T(2,128)S(1)} %get-tuple-element.374, f32[2,2,2,128]{3,2,1,0:T(2,128)S(1)} %get-tuple-element.342, ...), kind=kLoop, calls=%fused_computation.399 | loop fusion | flops 6288384 | bytes 86016 | tf_op jit(solution)/shard_map/reduce_sum | solution.py:85
  98.1 2.2 %fusion.335 = (f32[2,2,2,128]{3,2,1,0:T(2,128)S(1)}, f32[2,2,2,128]{3,2,1,0:T(2,128)S(1)}, f32[2,2,2,128]{3,2,1,0:T(2,128)S(1)}) fusion(f32[2,2,2,128]{3,2,1,0:T(2,128)S(1)} %get-tuple-element.263, f32[2,2,2,128]{3,2,1,0:T(2,128)S(1)} %get-tuple-element.269, f32[2,2,2,128]{3,2,1,0:T(2,128)S(1)} %get-tuple-element.342, ...), kind=kLoop, calls=%fused_computation.687 | loop fusion | flops 6288384 | bytes 86016 | tf_op jit(solution)/shard_map/reduce_sum | solution.py:85
  102.6 2.2 %fusion.431 = (f32[2,2,2,128]{3,2,1,0:T(2,128)S(1)}, f32[2,2,2,128]{3,2,1,0:T(2,128)S(1)}, f32[2,2,2,128]{3,2,1,0:T(2,128)S(1)}) fusion(f32[2,2,2,128]{3,2,1,0:T(2,128)S(1)} %get-tuple-element.290, f32[2,2,2,128]{3,2,1,0:T(2,128)S(1)} %get-tuple-element.296, f32[2,2,2,128]{3,2,1,0:T(2,128)S(1)} %get-tuple-element.342, ...), kind=kLoop, calls=%fused_computation.783 | loop fusion | flops 6288384 | bytes 86016 | tf_op jit(solution)/shard_map/reduce_sum | solution.py:85
  104.8 2.2 %fusion.287 = (f32[2,2,2,128]{3,2,1,0:T(2,128)S(1)}, f32[2,2,2,128]{3,2,1,0:T(2,128)S(1)}, f32[2,2,2,128]{3,2,1,0:T(2,128)S(1)}) fusion(f32[2,2,2,128]{3,2,1,0:T(2,128)S(1)} %get-tuple-element.299, f32[2,2,2,128]{3,2,1,0:T(2,128)S(1)} %get-tuple-element.305, f32[2,2,2,128]{3,2,1,0:T(2,128)S(1)} %get-tuple-element.342, ...), kind=kLoop, calls=%fused_computation.639 | loop fusion | flops 6288384 | bytes 86016 | tf_op jit(solution)/shard_map/reduce_sum | solution.py:85
  107.7 2.2 %fusion.415 = (f32[2,2,2,128]{3,2,1,0:T(2,128)S(1)}, f32[2,2,2,128]{3,2,1,0:T(2,128)S(1)}, f32[2,2,2,128]{3,2,1,0:T(2,128)S(1)}) fusion(f32[2,2,2,128]{3,2,1,0:T(2,128)S(1)} %get-tuple-element.178, f32[2,2,2,128]{3,2,1,0:T(2,128)S(1)} %get-tuple-element.184, f32[2,2,2,128]{3,2,1,0:T(2,128)S(1)} %get-tuple-element.342, ...), kind=kLoop, calls=%fused_computation.767 | loop fusion | flops 6288384 | bytes 86016 | tf_op jit(solution)/shard_map/reduce_sum | solution.py:85
  110.0 2.2 %fusion.367 = (f32[2,2,2,128]{3,2,1,0:T(2,128)S(1)}, f32[2,2,2,128]{3,2,1,0:T(2,128)S(1)}, f32[2,2,2,128]{3,2,1,0:T(2,128)S(1)}) fusion(f32[2,2,2,128]{3,2,1,0:T(2,128)S(1)} %get-tuple-element.187, f32[2,2,2,128]{3,2,1,0:T(2,128)S(1)} %get-tuple-element.193, f32[2,2,2,128]{3,2,1,0:T(2,128)S(1)} %get-tuple-element.342, ...), kind=kLoop, calls=%fused_computation.719 | loop fusion | flops 6288384 | bytes 86016 | tf_op jit(solution)/shard_map/reduce_sum | solution.py:85
  112.2 3.4 %fusion.31 = (f32[2,2,2,128]{3,2,1,0:T(2,128)S(1)}, f32[2,2,2,128]{3,2,1,0:T(2,128)S(1)}, f32[2,2,2,128]{3,2,1,0:T(2,128)S(1)}, f32[2,2,2,128]{3,2,1,0:T(2,128)S...) fusion(f32[2,2,2,128]{3,2,1,0:T(2,128)S(1)} %get-tuple-element.249, ...), kind=kLoop, calls=%fused_computation.383 | loop fusion | flops 12576768 | bytes 98304 | tf_op jit(solution)/shard_map/reduce_sum | solution.py:85
  115.6 2.2 %fusion.127 = (f32[2,2,2,128]{3,2,1,0:T(2,128)S(1)}, f32[2,2,2,128]{3,2,1,0:T(2,128)S(1)}, f32[2,2,2,128]{3,2,1,0:T(2,128)S(1)}) fusion(f32[2,2,2,128]{3,2,1,0:T(2,128)S(1)} %get-tuple-element.235, f32[2,2,2,128]{3,2,1,0:T(2,128)S(1)} %get-tuple-element.241, f32[2,2,2,128]{3,2,1,0:T(2,128)S(1)} %get-tuple-element.342, ...), kind=kLoop, calls=%fused_computation.479 | loop fusion | flops 6288384 | bytes 86016 | tf_op jit(solution)/shard_map/reduce_sum | solution.py:85
  117.8 2.2 %fusion.79 = (f32[2,2,2,128]{3,2,1,0:T(2,128)S(1)}, f32[2,2,2,128]{3,2,1,0:T(2,128)S(1)}, f32[2,2,2,128]{3,2,1,0:T(2,128)S(1)}) fusion(f32[2,2,2,128]{3,2,1,0:T(2,128)S(1)} %get-tuple-element.242, f32[2,2,2,128]{3,2,1,0:T(2,128)S(1)} %get-tuple-element.246, f32[2,2,2,128]{3,2,1,0:T(2,128)S(1)} %get-tuple-element.342, ...), kind=kLoop, calls=%fused_computation.431 | loop fusion | flops 6288384 | bytes 86016 | tf_op jit(solution)/shard_map/reduce_sum | solution.py:85
  120.1 2.2 %fusion.223 = (f32[2,2,2,128]{3,2,1,0:T(2,128)S(1)}, f32[2,2,2,128]{3,2,1,0:T(2,128)S(1)}, f32[2,2,2,128]{3,2,1,0:T(2,128)S(1)}) fusion(f32[2,2,2,128]{3,2,1,0:T(2,128)S(1)} %get-tuple-element.216, f32[2,2,2,128]{3,2,1,0:T(2,128)S(1)} %get-tuple-element.222, f32[2,2,2,128]{3,2,1,0:T(2,128)S(1)} %get-tuple-element.342, ...), kind=kLoop, calls=%fused_computation.575 | loop fusion | flops 6288384 | bytes 86016 | tf_op jit(solution)/shard_map/reduce_sum | solution.py:85
  124.6 2.2 %fusion.319 = (f32[2,2,2,128]{3,2,1,0:T(2,128)S(1)}, f32[2,2,2,128]{3,2,1,0:T(2,128)S(1)}, f32[2,2,2,128]{3,2,1,0:T(2,128)S(1)}) fusion(f32[2,2,2,128]{3,2,1,0:T(2,128)S(1)} %get-tuple-element.197, f32[2,2,2,128]{3,2,1,0:T(2,128)S(1)} %get-tuple-element.203, f32[2,2,2,128]{3,2,1,0:T(2,128)S(1)} %get-tuple-element.342, ...), kind=kLoop, calls=%fused_computation.671 | loop fusion | flops 6288384 | bytes 86016 | tf_op jit(solution)/shard_map/reduce_sum | solution.py:85
  126.8 2.2 %fusion.271 = (f32[2,2,2,128]{3,2,1,0:T(2,128)S(1)}, f32[2,2,2,128]{3,2,1,0:T(2,128)S(1)}, f32[2,2,2,128]{3,2,1,0:T(2,128)S(1)}) fusion(f32[2,2,2,128]{3,2,1,0:T(2,128)S(1)} %get-tuple-element.206, f32[2,2,2,128]{3,2,1,0:T(2,128)S(1)} %get-tuple-element.212, f32[2,2,2,128]{3,2,1,0:T(2,128)S(1)} %get-tuple-element.342, ...), kind=kLoop, calls=%fused_computation.623 | loop fusion | flops 6288384 | bytes 86016 | tf_op jit(solution)/shard_map/reduce_sum | solution.py:85
  129.0 2.2 %fusion.351 = (f32[2,2,2,128]{3,2,1,0:T(2,128)S(1)}, f32[2,2,2,128]{3,2,1,0:T(2,128)S(1)}, f32[2,2,2,128]{3,2,1,0:T(2,128)S(1)}) fusion(f32[2,2,2,128]{3,2,1,0:T(2,128)S(1)} %get-tuple-element.116, f32[2,2,2,128]{3,2,1,0:T(2,128)S(1)} %get-tuple-element.122, f32[2,2,2,128]{3,2,1,0:T(2,128)S(1)} %get-tuple-element.342, ...), kind=kLoop, calls=%fused_computation.703 | loop fusion | flops 6288384 | bytes 86016 | tf_op jit(solution)/shard_map/reduce_sum | solution.py:85
  131.3 2.2 %fusion.303 = (f32[2,2,2,128]{3,2,1,0:T(2,128)S(1)}, f32[2,2,2,128]{3,2,1,0:T(2,128)S(1)}, f32[2,2,2,128]{3,2,1,0:T(2,128)S(1)}) fusion(f32[2,2,2,128]{3,2,1,0:T(2,128)S(1)} %get-tuple-element.125, f32[2,2,2,128]{3,2,1,0:T(2,128)S(1)} %get-tuple-element.131, f32[2,2,2,128]{3,2,1,0:T(2,128)S(1)} %get-tuple-element.342, ...), kind=kLoop, calls=%fused_computation.655 | loop fusion | flops 6288384 | bytes 86016 | tf_op jit(solution)/shard_map/reduce_sum | solution.py:85
  133.5 2.2 %fusion.159 = (f32[2,2,2,128]{3,2,1,0:T(2,128)S(1)}, f32[2,2,2,128]{3,2,1,0:T(2,128)S(1)}, f32[2,2,2,128]{3,2,1,0:T(2,128)S(1)}) fusion(f32[2,2,2,128]{3,2,1,0:T(2,128)S(1)} %get-tuple-element.154, f32[2,2,2,128]{3,2,1,0:T(2,128)S(1)} %get-tuple-element.160, f32[2,2,2,128]{3,2,1,0:T(2,128)S(1)} %get-tuple-element.342, ...), kind=kLoop, calls=%fused_computation.511 | loop fusion | flops 6288384 | bytes 86016 | tf_op jit(solution)/shard_map/reduce_sum | solution.py:85
  138.0 2.2 %fusion.63 = (f32[2,2,2,128]{3,2,1,0:T(2,128)S(1)}, f32[2,2,2,128]{3,2,1,0:T(2,128)S(1)}, f32[2,2,2,128]{3,2,1,0:T(2,128)S(1)}) fusion(f32[2,2,2,128]{3,2,1,0:T(2,128)S(1)} %get-tuple-element.171, f32[2,2,2,128]{3,2,1,0:T(2,128)S(1)} %get-tuple-element.174, f32[2,2,2,128]{3,2,1,0:T(2,128)S(1)} %get-tuple-element.342, ...), kind=kLoop, calls=%fused_computation.415 | loop fusion | flops 6288384 | bytes 86016 | tf_op jit(solution)/shard_map/reduce_sum | solution.py:85
  140.2 2.5 %fusion.255 = (f32[2,2,2,128]{3,2,1,0:T(2,128)S(1)}, f32[2,2,2,128]{3,2,1,0:T(2,128)S(1)}, f32[2,2,2,128]{3,2,1,0:T(2,128)S(1)}) fusion(f32[2,2,2,128]{3,2,1,0:T(2,128)S(1)} %get-tuple-element.135, f32[2,2,2,128]{3,2,1,0:T(2,128)S(1)} %get-tuple-element.141, f32[2,2,2,128]{3,2,1,0:T(2,128)S(1)} %get-tuple-element.342, ...), kind=kLoop, calls=%fused_computation.607 | loop fusion | flops 6288384 | bytes 86016 | tf_op jit(solution)/shard_map/reduce_sum | solution.py:85
  142.7 2.2 %fusion.207 = (f32[2,2,2,128]{3,2,1,0:T(2,128)S(1)}, f32[2,2,2,128]{3,2,1,0:T(2,128)S(1)}, f32[2,2,2,128]{3,2,1,0:T(2,128)S(1)}) fusion(f32[2,2,2,128]{3,2,1,0:T(2,128)S(1)} %get-tuple-element.144, f32[2,2,2,128]{3,2,1,0:T(2,128)S(1)} %get-tuple-element.150, f32[2,2,2,128]{3,2,1,0:T(2,128)S(1)} %get-tuple-element.342, ...), kind=kLoop, calls=%fused_computation.559 | loop fusion | flops 6288384 | bytes 86016 | tf_op jit(solution)/shard_map/reduce_sum | solution.py:85
  144.9 2.2 %fusion.447 = (f32[2,2,2,128]{3,2,1,0:T(2,128)S(1)}, f32[2,2,2,128]{3,2,1,0:T(2,128)S(1)}, f32[2,2,2,128]{3,2,1,0:T(2,128)S(1)}) fusion(f32[2,2,2,128]{3,2,1,0:T(2,128)S(1)} %get-tuple-element.97, f32[2,2,2,128]{3,2,1,0:T(2,128)S(1)} %get-tuple-element.103, f32[2,2,2,128]{3,2,1,0:T(2,128)S(1)} %get-tuple-element.342, ...), kind=kLoop, calls=%fused_computation.799 | loop fusion | flops 6288384 | bytes 86016 | tf_op jit(solution)/shard_map/reduce_sum | solution.py:85
  (104 shorter events, 24.4 us)
Async XLA Ops:
  0.0 84.4 %copy-start = (f32[128,128]{1,0:T(8,128)S(1)}, f32[128,128]{1,0:T(8,128)}, u32[]{:S(2)}) copy-start(f32[128,128]{1,0:T(8,128)} %param.13) | copy-start | bytes 196612
  0.8 0.7 copy-start.1
  0.8 0.7 copy-start.2
  1.6 11.1 %collective-permute-start = (f32[9,1,2,2,128]{4,3,2,1,0:T(2,128)S(1)}, f32[9,1,2,2,128]{4,3,2,1,0:T(2,128)S(1)}, u32[]{:S(2)}, u32[]{:S(2)}) collective-permute-start(f32[9,1,2,2,128]{4,3,2,1,0:T(2,128)S(1)} %get-tuple-element.336), channel_id=1, source_target_pairs={{0,16},{16,0},{1,17},{17,1},{2,18},{18,2},{3,19},{19,3},{4,20},{20... | collective-permute-start | bytes 55304 | tf_op jit(solution)/shard_map/ppermute | solution.py:18
  4.6 8.1 %collective-permute-start.1 = (f32[9,1,2,2,128]{4,3,2,1,0:T(2,128)S(1)}, f32[9,1,2,2,128]{4,3,2,1,0:T(2,128)S(1)}, u32[]{:S(2)}, u32[]{:S(2)}) collective-permute-start(f32[9,1,2,2,128]{4,3,2,1,0:T(2,128)S(1)} %get-tuple-element.337), channel_id=1, source_target_pairs={{16,0},{0,16},{17,1},{1,17},{18,2},{2,18},{19,3},{3,19},{20,4},{4,... | collective-permute-start | bytes 55304 | tf_op jit(solution)/shard_map/ppermute | solution.py:19
  4.7 0.7 copy-start.5
  4.7 0.7 copy-start.4
  5.4 0.7 copy-start.3
  12.8 76.6 %collective-permute-start.2 = (f32[9,4,1,2,128]{4,3,2,1,0:T(2,128)S(1)}, f32[9,4,1,2,128]{4,3,2,1,0:T(2,128)S(1)}, u32[]{:S(2)}, u32[]{:S(2)}) collective-permute-start(f32[9,4,1,2,128]{4,3,2,1,0:T(2,128)S(1)} %get-tuple-element.316), channel_id=1, source_target_pairs={{0,4},{4,8},{8,12},{12,0},{1,5},{5,9},{9,13},{13,1},{2,6},{6,10},{... | collective-permute-start | bytes 110600 | tf_op jit(solution)/shard_map/ppermute | solution.py:18
  12.9 76.5 %collective-permute-start.3 = (f32[9,4,1,2,128]{4,3,2,1,0:T(2,128)S(1)}, f32[9,4,1,2,128]{4,3,2,1,0:T(2,128)S(1)}, u32[]{:S(2)}, u32[]{:S(2)}) collective-permute-start(f32[9,4,1,2,128]{4,3,2,1,0:T(2,128)S(1)} %get-tuple-element.317), channel_id=1, source_target_pairs={{4,0},{8,4},{12,8},{0,12},{5,1},{9,5},{13,9},{1,13},{6,2},{10,6},{... | collective-permute-start | bytes 110600 | tf_op jit(solution)/shard_map/ppermute | solution.py:19
  89.8 17.3 %collective-permute-start.4 = (f32[9,4,4,1,128]{4,3,2,1,0:T(1,128)S(1)}, f32[9,4,4,1,128]{4,3,2,1,0:T(1,128)S(1)}, u32[]{:S(2)}, u32[]{:S(2)}) collective-permute-start(f32[9,4,4,1,128]{4,3,2,1,0:T(1,128)S(1)} %get-tuple-element.258), channel_id=1, source_target_pairs={{0,1},{1,2},{2,3},{3,0},{4,5},{5,6},{6,7},{7,4},{8,9},{9,10},{10,1... | collective-permute-start | bytes 221192 | tf_op jit(solution)/shard_map/ppermute | solution.py:18
  89.9 17.2 %collective-permute-start.5 = (f32[9,4,4,1,128]{4,3,2,1,0:T(1,128)S(1)}, f32[9,4,4,1,128]{4,3,2,1,0:T(1,128)S(1)}, u32[]{:S(2)}, u32[]{:S(2)}) collective-permute-start(f32[9,4,4,1,128]{4,3,2,1,0:T(1,128)S(1)} %get-tuple-element.259), channel_id=1, source_target_pairs={{1,0},{2,1},{3,2},{0,3},{5,4},{6,5},{7,6},{4,7},{9,8},{10,9},{11,1... | collective-permute-start | bytes 221192 | tf_op jit(solution)/shard_map/ppermute | solution.py:19
where the time goes:
time: 151 us; the launch traced here: 150 us
  other arithmetic  68.9 us (46%)
  blocking collectives  68.8 us (46%)
  starting transfers between devices  8.77 us (6%)
  local copies, waits for them, and re-layouts  2.35 us (2%)
    all_gather x1, blocking collectives, body(): piece = lax.all_gather(moments, ('gx', 'gy', 'gz'), axis=0, tiled=True)  68.8 us
    reduce_sum x26, other arithmetic, pair_forces(): jnp.sum(first_coef * separation[column] + second_coef * source[3 + column...  59.4 us
    ppermute x3, starting transfers between devices, padded_2(): after = lax.ppermute(first, axis, down)  5.62 us
    sub x1, other arithmetic, crossed(): left[1] * right[2] - left[2] * right[1]  3.75 us
    ppermute x3, starting transfers between devices, padded_2(): before = lax.ppermute(last, axis, up)  3.15 us
  transfers between devices with their start and end apart: 6, of which 0 were waited for; matrix products, arithmetic and copies ran while one was open for 17% of the time, Pallas kernels for 0%

commit v1 on v0

v1 whole, which is shorter than its diff:
```python
import functools
import itertools
import math

import jax
import jax.numpy as jnp
import numpy as np
from jax import lax
from jax.experimental import pallas as pl
from jax.experimental.pallas import tpu as pltpu
from jax.sharding import PartitionSpec as P

core_square = 0.0625
near_scale = 0.01
highest = lax.Precision.HIGHEST
f32 = jnp.float32
bf16 = jnp.bfloat16
slots = 128
cells = 8
features = 64
forms = 4


def exponent_list():
    result = []
    for first in range(5):
        for second in range(5 - first):
            for third in range(5 - first - second):
                result.append((first, second, third))
    return result


def monomials(relative):
    powers = []
    for base in relative:
        square = base * base
        powers.append([None, base, square, square * base, square * square])
    result = []
    for triple in exponent_list():
        factors = [powers[axis][power] for axis, power in enumerate(triple) if power]
        result.append(functools.reduce(lambda a, b: a * b, factors) if factors else None)
    return result


def crossed(left, right):
    return [
        left[1] * right[2] - left[2] * right[1],
        left[2] * right[0] - left[0] * right[2],
        left[0] * right[1] - left[1] * right[0],
    ]


def dotted(left, right):
    return left[0] * right[0] + left[1] * right[1] + left[2] * right[2]


def split(value, parts):
    result = []
    for _ in range(parts):
        part = value.astype(bf16).astype(f32)
        result.append(part)
        value = value - part
    return result


def by_cell(scalars):
    row = lax.broadcasted_iota(jnp.int32, (cells, slots), 0)
    result = jnp.full((cells, slots), scalars[0, 0, 0])
    for cell in range(1, cells):
        result = jnp.where(row == cell, scalars[cell // 4, cell // 2 % 2, cell % 2], result)
    return result


def prepare_kernel(counts, offsets, lines, burgers, translation, out, after, before, alone):
    slot = lax.broadcasted_iota(jnp.int32, (cells, slots), 1)
    mask = (slot < by_cell(counts)).astype(f32)
    place = [offsets[axis] for axis in range(3)]
    line = [lines[axis] for axis in range(3)]
    charge = [burgers[axis] * mask for axis in range(3)]
    for axis in range(3):
        out[axis] = place[axis]
        out[3 + axis] = line[axis]
        out[6 + axis] = charge[axis]
    strength = crossed(charge, line)
    poly = monomials(place)
    moments = jnp.zeros((cells, slots), f32)
    for axis in range(3):
        for term, value in enumerate(poly):
            weighted = strength[axis] if value is None else value * strength[axis]
            total = jnp.sum(weighted, axis=1, keepdims=True)
            moments = jnp.where(slot == axis * len(poly) + term, total, moments)
    moved = jnp.dot(
        moments * (1.0 / slots), translation[...], precision=highest, preferred_element_type=f32
    )
    out[9] = moved
    alone[...] = moved
    for plane, message in ((0, after), (1, before)):
        for index in range(4):
            cell = 2 * index + plane
            message[0:9, index : index + 1, :] = out[0:9, cell : cell + 1, :]
        message[9] = moved[:4]
        message[10] = moved[4:]


def stack_rows(message, pieces, width):
    row = 0
    for piece in pieces:
        count = piece.shape[0]
        layer, start = (9 + row // width, row % width)
        message[layer, start : start + count, :] = piece
        row += count


def pack_x_kernel(own, high, low, *rest):
    middle, message = (rest[:-2], rest[-1])
    message[0:9, 0:8, :] = own[0:9]
    message[0:9, 8:12, :] = high[0:9]
    message[0:9, 12:16, :] = low[0:9]
    pieces = [own[9], high[9], high[10]] + [piece[...] for piece in middle] + [low[9], low[10]]
    stack_rows(message, pieces, 16)


def pack_y_kernel(starts, inner, outer, *rest):
    tails, messages, alone = (rest[: len(starts)], rest[-3:-1], rest[-1])
    for plane, message in enumerate(messages):
        for index, block in enumerate((inner, outer)):
            first = 8 * index
            for half in range(2):
                here, there = (first + 2 * half, 4 * half + 2 * plane)
                message[0:9, here : here + 2, :] = block[0:9, there : there + 2, :]
            for line in range(4):
                here, there = (first + 4 + line, 8 + 2 * line + plane)
                message[0:9, here : here + 1, :] = block[0:9, there : there + 1, :]
        layer = 9
        for start, tail in zip(starts, tails):
            for index in range(start, tail.shape[0]):
                message[layer] = tail[index]
                alone[layer - 9] = tail[index]
                layer += 1


def target_rows(place, line, charge):
    one = jnp.ones_like(place[0])
    rows = []
    for axis in range(3):
        high, middle, low = split(place[axis], 3)
        rows += [high, high, high, middle, middle, low]
    rows += split(dotted(place, place), 3)
    rows += [one, one, one]
    for axis in range(3):
        high, low = split(charge[axis], 2)
        rows += [high, high, low]
    rows += split(dotted(charge, place), 3)
    for first in range(3):
        for second in range(3):
            high, low = split(charge[first] * line[second], 2)
            rows += [high, high, low]
    return rows + [jnp.zeros_like(one)]


def source_rows(place, line, charge):
    one = jnp.ones_like(place[0])
    none = None
    radius, product, own, other = ([], [], [], [])
    for axis in range(3):
        high, middle, low = split(-2.0 * place[axis], 3)
        radius += [high, middle, low, high, middle, high]
        high, middle, low = split(charge[axis], 3)
        own += [high, middle, low, high, middle, high]
    product += [none] * 18
    other += [none] * 18
    radius += [one, one, one]
    own += [none] * 3
    product += [none] * 3
    other += [none] * 3
    radius += split(dotted(place, place) + core_square, 3)
    own += split(-dotted(charge, place), 3)
    product += [none] * 3
    other += [none] * 3
    for axis in range(3):
        high, low = split(-place[axis], 2)
        other += [high, low, high]
    other += [one, one, one]
    radius += [none] * 12
    own += [none] * 12
    product += [none] * 12
    for first in range(3):
        for second in range(3):
            high, low = split(charge[first] * line[second], 2)
            product += [high, low, high]
    product += [none]
    radius += [none] * 28
    own += [none] * 28
    other += [none] * 28
    return [radius, product, own, other]


def moved_block(block, base):
    place = [block[axis] + base[axis] for axis in range(3)]
    return place, [block[3 + axis] for axis in range(3)], [block[6 + axis] for axis in range(3)]


def add_targets(block, base, targets, stage):
    for index, row in enumerate(target_rows(*moved_block(block, base))):
        stage[index * cells : (index + 1) * cells, :] = row
    for cell in range(cells):
        rows = stage[pl.ds(cell, features, stride=cells), :]
        targets[cell * slots : (cell + 1) * slots, :] = rows.T.astype(bf16)


def add_sources(block, base, columns, parts, positions, stage):
    place, line, charge = moved_block(block, base)
    for form, rows in enumerate(source_rows(place, line, charge)):
        used = [index for index, row in enumerate(rows) if row is not None]
        low, high = (min(used) // 16 * 16, -(-(max(used) + 1) // 16) * 16)
        for index in range(low, high):
            row = jnp.zeros((cells, slots), f32) if rows[index] is None else rows[index]
            stage[index * cells : (index + 1) * cells, :] = row
        for cell in range(cells):
            part = stage[pl.ds(low * cells + cell, high - low, stride=cells), :].astype(bf16)
            first = (positions[cell] * forms + form) * slots
            if low:
                columns[0:low, first : first + slots] = jnp.zeros((low, slots), bf16)
            columns[low:high, first : first + slots] = part
            if high < features:
                rest = jnp.zeros((features - high, slots), bf16)
                columns[high:features, first : first + slots] = rest
    for index, row in enumerate(place + line):
        stage[index * cells : (index + 1) * cells, :] = row
    for cell in range(cells):
        first = positions[cell] * 8
        parts[first : first + 8, :] = stage[pl.ds(cell, 8, stride=cells), :]


def pair_products(mine, columns, first, count):
    width = forms * slots
    start = pl.multiple_of(first * width, width)
    return jnp.dot(mine, columns[:, pl.ds(start, count * width)], preferred_element_type=f32)


def add_pairs(totals, value, parts, first, count, fresh):
    start = pl.multiple_of(first * 8, 8)
    sources = []
    for cell in range(count):
        rows = parts[pl.ds(start + cell * 8, 8), :]
        sources.append([jnp.broadcast_to(rows[i : i + 1], (8, slots)) for i in range(6)])
    for group in range(value.shape[0] // 8):
        here = slice(group * 8, group * 8 + 8)
        sums = [None] * 4
        for cell in range(count):
            radius, product, own, other = (
                value[here, (cell * forms + form) * slots : (cell * forms + form + 1) * slots]
                for form in range(forms)
            )
            inverse = lax.rsqrt(radius)
            square = inverse * inverse
            cube = inverse * square
            along = product * cube
            across = (own * other) * (square * cube)
            terms = [along * sources[cell][a] + across * sources[cell][3 + a] for a in range(3)]
            terms.append(along)
            sums = [term if s is None else s + term for s, term in zip(sums, terms)]
        for index in range(4):
            place = slice(index * slots + group * 8, index * slots + group * 8 + 8)
            totals[place, :] = sums[index] if fresh else totals[place, :] + sums[index]


def own_cells():
    return [(x + 1, y + 1, z + 1) for x in range(2) for y in range(2) for z in range(2)]


def z_cells():
    return [(x + 1, y + 1, z) for z in (3, 0) for x in range(2) for y in range(2)]


def x_cells():
    near = [(x, y + 1, z + 1) for x in (3, 0) for y in range(2) for z in range(2)]
    return [near, [(x, y + 1, z) for z in (3, 0) for x in (3, 0) for y in range(2)]]


def y_cells(y):
    result = []
    for xs in ((1, 2), (3, 0)):
        cell = [(x, y, z + 1) for x in xs for z in range(2)]
        result.append(cell + [(x, y, z) for z in (3, 0) for x in xs])
    return result


def base_of(places):
    row = lax.broadcasted_iota(jnp.int32, (cells, slots), 0)
    result = []
    for axis in range(3):
        value = jnp.full((cells, slots), places[0][axis] - 1.5, f32)
        for cell in range(1, cells):
            if places[cell][axis] != places[0][axis]:
                value = jnp.where(row == cell, places[cell][axis] - 1.5, value)
        result.append(value)
    return result


def near_sums(targets, groups, runs_of, earlier, columns, parts, stage, totals, mixed, gathered):
    for block, places, positions in groups:
        add_sources(block, base_of(places), columns, parts, positions, stage)

    def one_target(target, carry):
        mine = targets[pl.ds(pl.multiple_of(target * slots, slots), slots), :]
        runs = runs_of(target // 4, target // 2 % 2, target % 2)
        value = pair_products(mine, columns, *runs[0])
        for index, run in enumerate(runs):
            later = None
            if index + 1 < len(runs):
                later = pair_products(mine, columns, *runs[index + 1])
            add_pairs(totals, value, parts, *run, index == 0)
            value = later
        lane = lax.broadcasted_iota(jnp.int32, (slots, slots), 1)
        for index in range(4):
            total = jnp.sum(totals[index * slots : (index + 1) * slots, :], axis=1, keepdims=True)
            mixed[...] = jnp.where(lane == index * cells + target, total, mixed[...])
        return carry

    mixed[...] = jnp.zeros((slots, slots), f32)
    lax.fori_loop(0, cells, one_target, 0)
    result = mixed[...].T[: 4 * cells, :]
    gathered[...] = result if earlier is None else result + earlier[...]


def rows_of(block, first=0):
    return [block[axis, first : first + cells, :] for axis in range(9)]


def own_kernel(own, message, targets, out, *scratch):
    add_targets(rows_of(own), base_of(own_cells()), targets, scratch[2])
    groups = [(rows_of(own), own_cells(), list(range(8)))]

    def runs(x, y, z):
        return [(first, 2) for first in (0, 2, 4, 6)]

    near_sums(targets, groups, runs, None, *scratch, out)


def z_kernel(targets, halo, earlier, out, *scratch):
    groups = [(rows_of(halo, 8), z_cells(), list(range(8)))]

    def runs(x, y, z):
        return [(4 * (1 - z) + first, 2) for first in (0, 2)]

    near_sums(targets, groups, runs, earlier, *scratch, out)


def x_kernel(targets, halo, message, earlier, out, *scratch):
    groups = []
    for index, places in enumerate(x_cells()):
        positions = [(0 if x == 3 else 8) + 2 * z + y - 1 for x, y, z in places]
        groups.append((rows_of(halo, 8 * index), places, positions))

    def runs(x, y, z):
        return [(8 * (1 - x) + 2 * z + first, 2) for first in (0, 2, 4)]

    near_sums(targets, groups, runs, earlier, *scratch, out)


def y_kernel(
    starts, stress, mobility, counts, own, targets, high, low, earlier, weights_far, *rest
):
    tails, out, scratch = (rest[: len(starts)], rest[len(starts)], rest[len(starts) + 1 :])
    gathered = scratch[-1]
    groups = []
    for block, side in ((high, 3), (low, 0)):
        for index, places in enumerate(y_cells(side)):
            positions = [(16 if side else 0) + 4 * x + z for x, y, z in places]
            groups.append((rows_of(block, 8 * index), places, positions))

    def runs(x, y, z):
        return [(16 * y + 4 * (x + line) + z, 3) for line in range(3)]

    near_sums(targets, groups, runs, earlier, *scratch)
    sums_of = [gathered[index * cells : (index + 1) * cells, :] for index in range(4)]
    local = [tail[index] for start, tail in zip(starts, tails) for index in range(start, tail.shape[0])]
    coefficients = jnp.dot(
        weights_far[...],
        jnp.concatenate(local, axis=0),
        precision=highest,
        preferred_element_type=f32,
    )
    place = [own[axis] for axis in range(3)]
    line = [own[3 + axis] for axis in range(3)]
    charge = [own[6 + axis] for axis in range(3)]
    base = base_of(own_cells())
    poly = monomials(place)
    mask = (lax.broadcasted_iota(jnp.int32, (cells, slots), 1) < by_cell(counts)).astype(f32)
    stressed = [
        stress[a, 0] * charge[0] + stress[a, 1] * charge[1] + stress[a, 2] * charge[2]
        for a in range(3)
    ]
    applied = crossed(stressed, line)
    force = []
    for axis in range(3):
        at = place[axis] + base[axis]
        near = sums_of[axis] - at * sums_of[3]
        far = jnp.zeros((cells, slots), f32)
        for term, value in enumerate(poly):
            column = axis * len(poly) + term
            coefficient = coefficients[:, column : column + 1]
            far = far + (coefficient if value is None else coefficient * value)
        force.append(near_scale * near + far * mask + applied[axis])
    ratio = dotted(force, line) / jnp.maximum(dotted(line, line), 1.0)
    scale = by_cell(mobility) * mask
    for axis in range(3):
        out[axis] = scale * (force[axis] - ratio * line[axis])


def far_weights(sizes):
    corners = list(itertools.product(range(2), repeat=3))
    result = []
    for here in corners:
        line = []
        for y, x, z in itertools.product(range(sizes[1]), range(sizes[0]), range(sizes[2])):
            for there in corners:
                gaps = []
                for axis, step in enumerate((x, y, z)):
                    extent = 2 * sizes[axis]
                    gap = (2 * step + there[axis] - here[axis]) % extent
                    gaps.append(min(gap, extent - gap))
                apart = math.sqrt(sum(gap * gap for gap in gaps))
                line.append(1.0 / apart if max(gaps) > 1 else 0.0)
        result.append(line)
    return np.asarray(result, np.float32)


def shifted(value, axis, step):
    count = lax.axis_size(axis)
    return lax.ppermute(value, axis, [(i, (i - step) % count) for i in range(count)])


def near_call(kernel, name, count, pairs, scalars, arrays, shape, last=False):
    vmem = pl.BlockSpec(memory_space=pltpu.VMEM)
    smem = pl.BlockSpec(memory_space=pltpu.SMEM)
    scratch = [
        pltpu.VMEM((features, count * forms * slots), bf16),
        pltpu.VMEM((count * 8, slots), f32),
        pltpu.VMEM((features * cells, slots), f32),
        pltpu.VMEM((4 * slots, slots), f32),
        pltpu.VMEM((slots, slots), f32),
    ]
    if last:
        scratch.append(pltpu.VMEM((4 * cells, slots), f32))
    return pl.pallas_call(
        kernel,
        out_shape=shape,
        in_specs=[smem] * len(scalars) + [vmem] * len(arrays),
        out_specs=jax.tree.map(lambda leaf: vmem, shape),
        scratch_shapes=scratch,
        compiler_params=pltpu.CompilerParams(vmem_limit_bytes=8 * 1024 * 1024),
        cost_estimate=pl.CostEstimate(
            flops=pairs * slots * slots * 8000, bytes_accessed=1 << 20, transcendentals=0
        ),
        name=name,
    )(*scalars, *arrays)


def body(offsets, lines, burgers, counts, mobility, stress, translation):
    sizes = [lax.axis_size(axis) for axis in ("gx", "gy", "gz")]
    flat = [value.reshape(3, cells, slots) for value in (offsets, lines, burgers)]
    vmem = pl.BlockSpec(memory_space=pltpu.VMEM)
    smem = pl.BlockSpec(memory_space=pltpu.SMEM)
    message = jax.ShapeDtypeStruct((11, 4, slots), f32)
    block = jax.ShapeDtypeStruct((10, cells, slots), f32)
    own, up, down, moments = pl.pallas_call(
        prepare_kernel,
        out_shape=(block, message, message, jax.ShapeDtypeStruct((cells, slots), f32)),
        in_specs=[smem] + [vmem] * 4,
        out_specs=(vmem,) * 4,
        compiler_params=pltpu.CompilerParams(vmem_limit_bytes=4 * 1024 * 1024),
        name="prepare",
    )(counts, *flat, translation)
    high = shifted(up, "gz", 1)
    low = shifted(down, "gz", -1)
    middle = [shifted(moments, "gz", step) for step in range(2, sizes[2] - 1)]
    sums = jax.ShapeDtypeStruct((4 * cells, slots), f32)
    both = (jax.ShapeDtypeStruct((cells * slots, features), bf16), sums)
    targets, partial = near_call(own_kernel, "near_own", 8, 64, [], [own, up], both)
    message = pl.pallas_call(
        pack_x_kernel,
        out_shape=jax.ShapeDtypeStruct((9 + sizes[2] // 2, 16, slots), f32),
        in_specs=[vmem] * (4 + len(middle)),
        out_specs=vmem,
        compiler_params=pltpu.CompilerParams(vmem_limit_bytes=4 * 1024 * 1024),
        name="pack_x",
    )(own, high, low, *middle, partial)
    if sizes[0] == 2:
        outer = shifted(message, "gx", 1)
        starts, tails = ([9, 9], [message, outer])
    else:
        moments = message[9:].reshape(-1, slots)
        tail = moments.reshape(-1, 8, slots)
        planes = []
        for plane in (0, 1):
            part = [
                message[:9, :8].reshape(9, 2, 4, slots)[:, plane],
                message[:9, 8:].reshape(9, 2, 2, 2, slots)[:, :, plane].reshape(9, 4, slots),
            ]
            planes.append(jnp.concatenate([jnp.concatenate(part, axis=1), tail], axis=0))
        after = shifted(planes[0], "gx", 1)
        before = shifted(planes[1], "gx", -1)
        others = [shifted(moments, "gx", step) for step in range(2, sizes[0] - 1)]
        both = [after[:9], before[:9]]
        sides = [value[:, 4:].reshape(9, 2, 1, 2, slots) for value in both]
        sides = jnp.concatenate(sides, axis=2).reshape(9, 8, slots)
        outer = jnp.concatenate([value[:, :4] for value in both] + [sides], axis=1)
        moments = jnp.concatenate(
            [moments, after[9:].reshape(-1, slots)] + others + [before[9:].reshape(-1, slots)],
            axis=0,
        )
        starts, tails = ([0], [moments.reshape(-1, 16, slots)])
    partial = near_call(z_kernel, "near_z", 8, 32, [], [targets, message, partial], sums)
    layers = 9 + sum(tail.shape[0] - start for start, tail in zip(starts, tails))
    face = jax.ShapeDtypeStruct((layers, 16, slots), f32)
    up, down, moments = pl.pallas_call(
        functools.partial(pack_y_kernel, starts),
        out_shape=(face, face, jax.ShapeDtypeStruct((layers - 9, 16, slots), f32)),
        in_specs=[vmem] * (3 + len(tails)),
        out_specs=(vmem,) * 3,
        compiler_params=pltpu.CompilerParams(vmem_limit_bytes=4 * 1024 * 1024),
        name="pack_y",
    )(message, outer, *tails, partial)
    high = shifted(up, "gy", 1)
    low = shifted(down, "gy", -1)
    middle = [shifted(moments, "gy", step) for step in range(2, sizes[1] - 1)]
    partial = near_call(x_kernel, "near_x", 16, 48, [], [targets, outer, up, partial], sums)
    starts = starts + [9] + [0] * len(middle) + [9]
    tails = tails + [high] + middle + [low]
    out = near_call(
        functools.partial(y_kernel, starts),
        "near_y",
        32,
        72,
        [stress, mobility, counts],
        [own, targets, high, low, partial, jnp.asarray(far_weights(sizes))] + tails,
        jax.ShapeDtypeStruct((3, cells, slots), f32),
        last=True,
    )
    return out.reshape(3, 2, 2, 2, slots)


def solution(mesh):
    placed = (
        P(None, "gx", "gy", "gz", None),
        P(None, "gx", "gy", "gz", None),
        P(None, "gx", "gy", "gz", None),
        P("gx", "gy", "gz"),
        P("gx", "gy", "gz"),
        P(),
        P(),
    )
    return jax.shard_map(
        body, mesh=mesh, in_specs=placed, out_specs=P(None, "gx", "gy", "gz", None), check_vma=False
    )
```

time: 151 us -> 38.7 us (0.26)
  other arithmetic: 68.9 us -> 0 us
  blocking collectives: 68.8 us -> 0 us
  Pallas kernels: 0 us -> 21.7 us
  starting transfers between devices: 8.77 us -> 12.8 us
    all_gather x1 -> x0, blocking collectives: 68.8 us -> none  [body(): piece = lax.all_gather(moments, ('gx', 'gy', 'gz'), axis=0, tiled=True)]
    reduce_sum x27 -> x0, other arithmetic: 59.7 us -> none  [the longest x26 59.4 us: pair_forces(): jnp.sum(first_coef * separation[column] + second_coef * source[3 + column...]
    pallas_call x0 -> x7, Pallas kernels: none -> 21.7 us  [the longest x4 20.7 us: near_call(): pl.pallas_call(kernel, out_shape=shape, in_specs=[smem] * len(scalars) +...]
    sub x3 -> x0, other arithmetic: 5.69 us -> none  [the longest x1 3.75 us: crossed(): left[1] * right[2] - left[2] * right[1]]
    ppermute x6 -> x7, starting transfers between devices: 8.77 us -> 12.8 us  [shifted(): lax.ppermute(value, axis, [(i, (i - step) % count) for i in range(count)])]
    unnamed x15 -> x16, local copies, waits for them, and re-layouts: 1.32 us -> 3.65 us
    mul x16 -> x0, other arithmetic: 1.76 us -> none  [the longest x1 0.74 us: body(): charge = burgers * mask]
  transfers between devices with their start and end apart: 6 -> 7, of which waited for: 0 -> 0; matrix products, arithmetic and copies ran while one was open for 17% -> 0% of each run, Pallas kernels for 0% -> 34%
where the time goes in v1:
time: 38.7 us; the launch traced here: 38.3 us
  Pallas kernels  21.7 us (56%)
  starting transfers between devices  12.8 us (33%)
  local copies, waits for them, and re-layouts  3.65 us (9%)
    pallas_call x4, Pallas kernels, near_call(): pl.pallas_call(kernel, out_shape=shape, in_specs=[smem] * len(scalars) +...  20.7 us
    ppermute x7, starting transfers between devices, shifted(): lax.ppermute(value, axis, [(i, (i - step) % count) for i in range(count)])  12.8 us
    unnamed x16, local copies, waits for them, and re-layouts  3.65 us
    pallas_call x1, Pallas kernels, body(): pl.pallas_call(prepare_kernel, out_shape=(block, message, message, jax.Sh...  0.91 us
  transfers between devices with their start and end apart: 7, of which 0 were waited for; matrix products, arithmetic and copies ran while one was open for 0% of the time, Pallas kernels for 34%

profile of v1, /device:TPU:0, one launch (start us, length us, event | category | flops | bytes accessed | tf_op | source)
XLA Modules:
  0.0 38.3 jit_solution(2749799389521645285)
XLA Ops:
  0.0 0.7 %copy-done.4 = s32[2,2,2]{2,1,0:T(2,128)S(1)} copy-done((s32[2,2,2]{2,1,0:T(2,128)S(1)}, s32[2,2,2]{2,1,0:T(2,128)}, u32[]{:S(2)}) %copy-start.4) | copy-done | bytes 56
  0.7 0.8 %copy-done = f32[128,128]{1,0:T(8,128)S(1)} copy-done((f32[128,128]{1,0:T(8,128)S(1)}, f32[128,128]{1,0:T(8,128)}, u32[]{:S(2)}) %copy-start) | copy-done | bytes 65560
  1.5 0.7 %copy-done.1 = f32[3,2,2,2,128]{4,3,2,1,0:T(2,128)S(1)} copy-done((f32[3,2,2,2,128]{4,3,2,1,0:T(2,128)S(1)}, f32[3,2,2,2,128]{4,3,2,1,0:T(2,128)}, u32[]{:S(2)}) %copy-start.1) | copy-done | bytes 12312
  2.2 0.7 %copy-done.2 = f32[3,2,2,2,128]{4,3,2,1,0:T(2,128)S(1)} copy-done((f32[3,2,2,2,128]{4,3,2,1,0:T(2,128)S(1)}, f32[3,2,2,2,128]{4,3,2,1,0:T(2,128)}, u32[]{:S(2)}) %copy-start.2) | copy-done | bytes 12312
  2.9 0.7 %copy-done.3 = f32[3,2,2,2,128]{4,3,2,1,0:T(2,128)S(1)} copy-done((f32[3,2,2,2,128]{4,3,2,1,0:T(2,128)S(1)}, f32[3,2,2,2,128]{4,3,2,1,0:T(2,128)}, u32[]{:S(2)}) %copy-start.3) | copy-done | bytes 12312
  3.6 0.9 %prepare.1 = (f32[10,8,128]{2,1,0:T(8,128)S(1)}, f32[11,4,128]{2,1,0:T(4,128)S(1)}, f32[11,4,128]{2,1,0:T(4,128)S(1)}, f32[8,128]{1,0:T(8,128)S(1)}) custom-call(s32[2,2,2]{2,1,0:T(2,128)S(1)} %copy-done.4, f32[3,8,128]{2,1,0:T(8,128)S(1)} %bitcast.4, f32[3,8,128]{2,1,0:T(8,128)S(1)} %bitcast.5, f32[3,8,128]{2,1,0:T(8,128)S(1)} %bitcast.6, ...), custom_call_target="tpu_custom_call" | custom-call | tf_op jit(solution)/shard_map/prepare/pallas_call | solution.py:468
  4.6 4.0 %collective-permute-start.2 = (f32[8,128]{1,0:T(8,128)S(1)}, f32[8,128]{1,0:T(8,128)S(1)}, u32[]{:S(2)}, u32[]{:S(2)}) collective-permute-start(f32[8,128]{1,0:T(8,128)S(1)} %get-tuple-element.18), channel_id=1, source_target_pairs={{0,2},{1,3},{2,0},{3,1},{4,6},{5,7},{6,4},{7,5},{8,10},{9,11},{10,... | collective-permute-start | bytes 12296 | tf_op jit(solution)/shard_map/ppermute | solution.py:432
  8.6 1.6 %collective-permute-start.1 = (f32[11,4,128]{2,1,0:T(4,128)S(1)}, f32[11,4,128]{2,1,0:T(4,128)S(1)}, u32[]{:S(2)}, u32[]{:S(2)}) collective-permute-start(f32[11,4,128]{2,1,0:T(4,128)S(1)} %get-tuple-element.17), channel_id=1, source_target_pairs={{0,1},{1,2},{2,3},{3,0},{4,5},{5,6},{6,7},{7,4},{8,9},{9,10},{10,1... | collective-permute-start | bytes 67592 | tf_op jit(solution)/shard_map/ppermute | solution.py:432
  10.2 2.2 %collective-permute-start = (f32[11,4,128]{2,1,0:T(4,128)S(1)}, f32[11,4,128]{2,1,0:T(4,128)S(1)}, u32[]{:S(2)}, u32[]{:S(2)}) collective-permute-start(f32[11,4,128]{2,1,0:T(4,128)S(1)} %get-tuple-element.15.message), channel_id=1, source_target_pairs={{0,3},{1,0},{2,1},{3,2},{4,7},{5,4},{6,5},{7,6},{8,11},{9,8},{10,9... | collective-permute-start | bytes 67592 | tf_op jit(solution)/shard_map/ppermute | solution.py:432
  12.4 5.2 %near_own.1 = (bf16[1024,64]{1,0:T(8,128)(2,1)S(1)}, f32[32,128]{1,0:T(8,128)S(1)}) custom-call(f32[10,8,128]{2,1,0:T(8,128)S(1)} %get-tuple-element.14.own, f32[11,4,128]{2,1,0:T(4,128)S(1)} %get-tuple-element.15.message), custom_call_target="tpu_custom_call" | custom-call | flops 8388608000 | bytes 1048576 | tf_op jit(solution)/shard_map/near_own/pallas_call | solution.py:447
  17.6 0.0 collective-permute-done.2.rest_0_
  17.6 0.0 collective-permute-done.1.low
  17.6 1.6 %collective-permute-start.3 = (f32[11,16,128]{2,1,0:T(8,128)S(1)}, f32[11,16,128]{2,1,0:T(8,128)S(1)}, u32[]{:S(2)}, u32[]{:S(2)}) collective-permute-start(f32[11,16,128]{2,1,0:T(8,128)S(1)} %pack_x.1.halo.inner.rest_0_), channel_id=1, source_target_pairs={{0,16},{16,0},{1,17},{17,1},{2,18},{18,2},{3,19},{19,3},{4,20},{20... | collective-permute-start | bytes 270344 | tf_op jit(solution)/shard_map/ppermute | solution.py:432
  19.2 3.5 %near_z.1.rest_2_.earlier = f32[32,128]{1,0:T(8,128)S(1)} custom-call(bf16[1024,64]{1,0:T(8,128)(2,1)S(1)} %get-tuple-element.16.targets, f32[11,16,128]{2,1,0:T(8,128)S(1)} %pack_x.1.halo.inner.rest_0_, f32[32,128]{1,0:T(8,128)S(1)} %get-tuple-element.19.rest_1_.earlier), custom_call_target="tpu_custom_call" | custom-call | flops 4194304000 | bytes 1048576 | tf_op jit(solution)/shard_map/near_z/pallas_call | solution.py:447
  22.7 0.0 collective-permute-done.3.outer.rest_1_.halo
  22.7 0.1 pack_y.1
  22.8 1.6 %collective-permute-start.6 = (f32[4,16,128]{2,1,0:T(8,128)S(1)}, f32[4,16,128]{2,1,0:T(8,128)S(1)}, u32[]{:S(2)}, u32[]{:S(2)}) collective-permute-start(f32[4,16,128]{2,1,0:T(8,128)S(1)} %get-tuple-element.22), channel_id=1, source_target_pairs={{0,8},{4,12},{8,0},{12,4},{1,9},{5,13},{9,1},{13,5},{2,10},{6,14},... | collective-permute-start | bytes 98312 | tf_op jit(solution)/shard_map/ppermute | solution.py:432
  24.3 0.0 collective-permute-start.5
  24.4 1.7 %collective-permute-start.4 = (f32[13,16,128]{2,1,0:T(8,128)S(1)}, f32[13,16,128]{2,1,0:T(8,128)S(1)}, u32[]{:S(2)}, u32[]{:S(2)}) collective-permute-start(f32[13,16,128]{2,1,0:T(8,128)S(1)} %get-tuple-element.20.message), channel_id=1, source_target_pairs={{0,12},{4,0},{8,4},{12,8},{1,13},{5,1},{9,5},{13,9},{2,14},{6,2},{... | collective-permute-start | bytes 319496 | tf_op jit(solution)/shard_map/ppermute | solution.py:432
  26.1 4.4 %near_x.1.earlier = f32[32,128]{1,0:T(8,128)S(1)} custom-call(bf16[1024,64]{1,0:T(8,128)(2,1)S(1)} %get-tuple-element.16.targets, f32[11,16,128]{2,1,0:T(8,128)S(1)} %collective-permute-done.3.outer.rest_1_.halo, f32[13,16,128]{2,1,0:T(8,128)S(1)} %get-tuple-element.20.message, f32[32,128]{1,0:T(8,128)S(1)} %near_z.1.rest_2_.earlier), custom_call_target="tpu_custom_call" | custom-call | flops 6291456000 | bytes 1048576 | tf_op jit(solution)/shard_map/near_x/pallas_call | solution.py:447
  30.5 0.0 collective-permute-done.6.rest_3_
  30.5 0.0 collective-permute-done.5.low.rest_4_
  30.5 0.0 collective-permute-done.4.high.rest_2_
  30.6 7.7 %near_y.1 = f32[3,8,128]{2,1,0:T(8,128)} custom-call(f32[3,3]{1,0:T(4,128)S(1)} %copy-done.5, f32[2,2,2]{2,1,0:T(2,128)S(1)} %copy-done.6, s32[2,2,2]{2,1,0:T(2,128)S(1)} %copy-done.4, f32[10,8,128]{2,1,0:T(8,128)S(1)} %get-tuple-element.14.own, bf16[1024,64]{1,0:T(8,128)(2,1)S(1)} %get-tuple-element.16.targets, ...), custom_call_target="tpu_custom_call" | custom-call | flops 9437184000 | bytes 1048576 | tf_op jit(solution)/shard_map/near_y/pallas_call | solution.py:447
  (13 shorter events, 0.0 us)
Async XLA Ops:
  0.0 0.7 %copy-start.4 = (s32[2,2,2]{2,1,0:T(2,128)S(1)}, s32[2,2,2]{2,1,0:T(2,128)}, u32[]{:S(2)}) copy-start(s32[2,2,2]{2,1,0:T(2,128)} %counts.3) | copy-start | bytes 100
  0.7 0.8 %copy-start = (f32[128,128]{1,0:T(8,128)S(1)}, f32[128,128]{1,0:T(8,128)}, u32[]{:S(2)}) copy-start(f32[128,128]{1,0:T(8,128)} %translation.1) | copy-start | bytes 196612
  1.5 0.7 %copy-start.1 = (f32[3,2,2,2,128]{4,3,2,1,0:T(2,128)S(1)}, f32[3,2,2,2,128]{4,3,2,1,0:T(2,128)}, u32[]{:S(2)}) copy-start(f32[3,2,2,2,128]{4,3,2,1,0:T(2,128)} %param.8) | copy-start | bytes 36868
  2.2 0.7 %copy-start.2 = (f32[3,2,2,2,128]{4,3,2,1,0:T(2,128)S(1)}, f32[3,2,2,2,128]{4,3,2,1,0:T(2,128)}, u32[]{:S(2)}) copy-start(f32[3,2,2,2,128]{4,3,2,1,0:T(2,128)} %param.9) | copy-start | bytes 36868
  2.9 0.7 %copy-start.3 = (f32[3,2,2,2,128]{4,3,2,1,0:T(2,128)S(1)}, f32[3,2,2,2,128]{4,3,2,1,0:T(2,128)}, u32[]{:S(2)}) copy-start(f32[3,2,2,2,128]{4,3,2,1,0:T(2,128)} %param.10) | copy-start | bytes 36868
  4.6 13.0 %collective-permute-start.2 = (f32[8,128]{1,0:T(8,128)S(1)}, f32[8,128]{1,0:T(8,128)S(1)}, u32[]{:S(2)}, u32[]{:S(2)}) collective-permute-start(f32[8,128]{1,0:T(8,128)S(1)} %get-tuple-element.18), channel_id=1, source_target_pairs={{0,2},{1,3},{2,0},{3,1},{4,6},{5,7},{6,4},{7,5},{8,10},{9,11},{10,... | collective-permute-start | bytes 12296 | tf_op jit(solution)/shard_map/ppermute | solution.py:432
  8.6 9.0 %collective-permute-start.1 = (f32[11,4,128]{2,1,0:T(4,128)S(1)}, f32[11,4,128]{2,1,0:T(4,128)S(1)}, u32[]{:S(2)}, u32[]{:S(2)}) collective-permute-start(f32[11,4,128]{2,1,0:T(4,128)S(1)} %get-tuple-element.17), channel_id=1, source_target_pairs={{0,1},{1,2},{2,3},{3,0},{4,5},{5,6},{6,7},{7,4},{8,9},{9,10},{10,1... | collective-permute-start | bytes 67592 | tf_op jit(solution)/shard_map/ppermute | solution.py:432
  10.2 7.4 %collective-permute-start = (f32[11,4,128]{2,1,0:T(4,128)S(1)}, f32[11,4,128]{2,1,0:T(4,128)S(1)}, u32[]{:S(2)}, u32[]{:S(2)}) collective-permute-start(f32[11,4,128]{2,1,0:T(4,128)S(1)} %get-tuple-element.15.message), channel_id=1, source_target_pairs={{0,3},{1,0},{2,1},{3,2},{4,7},{5,4},{6,5},{7,6},{8,11},{9,8},{10,9... | collective-permute-start | bytes 67592 | tf_op jit(solution)/shard_map/ppermute | solution.py:432
  17.6 5.1 %collective-permute-start.3 = (f32[11,16,128]{2,1,0:T(8,128)S(1)}, f32[11,16,128]{2,1,0:T(8,128)S(1)}, u32[]{:S(2)}, u32[]{:S(2)}) collective-permute-start(f32[11,16,128]{2,1,0:T(8,128)S(1)} %pack_x.1.halo.inner.rest_0_), channel_id=1, source_target_pairs={{0,16},{16,0},{1,17},{17,1},{2,18},{18,2},{3,19},{19,3},{4,20},{20... | collective-permute-start | bytes 270344 | tf_op jit(solution)/shard_map/ppermute | solution.py:432
  22.8 7.7 %collective-permute-start.6 = (f32[4,16,128]{2,1,0:T(8,128)S(1)}, f32[4,16,128]{2,1,0:T(8,128)S(1)}, u32[]{:S(2)}, u32[]{:S(2)}) collective-permute-start(f32[4,16,128]{2,1,0:T(8,128)S(1)} %get-tuple-element.22), channel_id=1, source_target_pairs={{0,8},{4,12},{8,0},{12,4},{1,9},{5,13},{9,1},{13,5},{2,10},{6,14},... | collective-permute-start | bytes 98312 | tf_op jit(solution)/shard_map/ppermute | solution.py:432
  24.3 6.2 %collective-permute-start.5 = (f32[13,16,128]{2,1,0:T(8,128)S(1)}, f32[13,16,128]{2,1,0:T(8,128)S(1)}, u32[]{:S(2)}, u32[]{:S(2)}) collective-permute-start(f32[13,16,128]{2,1,0:T(8,128)S(1)} %get-tuple-element.21), channel_id=1, source_target_pairs={{0,4},{4,8},{8,12},{12,0},{1,5},{5,9},{9,13},{13,1},{2,6},{6,10},{... | collective-permute-start | bytes 319496 | tf_op jit(solution)/shard_map/ppermute | solution.py:432
  24.4 6.2 %copy-start.5 = (f32[3,3]{1,0:T(4,128)S(1)}, f32[3,3]{1,0:T(4,128)}, u32[]{:S(2)}) copy-start(f32[3,3]{1,0:T(4,128)} %stress.1) | copy-start | bytes 112
  24.4 6.2 %copy-start.6 = (f32[2,2,2]{2,1,0:T(2,128)S(1)}, f32[2,2,2]{2,1,0:T(2,128)}, u32[]{:S(2)}) copy-start(f32[2,2,2]{2,1,0:T(2,128)} %mobility.1) | copy-start | bytes 100
  24.4 6.2 %copy-start.7 = (f32[8,256]{1,0:T(8,128)S(1)}, f32[8,256]{1,0:T(8,128)}, u32[]{:S(2)}) copy-start(f32[8,256]{1,0:T(8,128)} %constant.2.clone.weights_far) | copy-start | bytes 24580
  24.4 6.2 %collective-permute-start.4 = (f32[13,16,128]{2,1,0:T(8,128)S(1)}, f32[13,16,128]{2,1,0:T(8,128)S(1)}, u32[]{:S(2)}, u32[]{:S(2)}) collective-permute-start(f32[13,16,128]{2,1,0:T(8,128)S(1)} %get-tuple-element.20.message), channel_id=1, source_target_pairs={{0,12},{4,0},{8,4},{12,8},{1,13},{5,1},{9,5},{13,9},{2,14},{6,2},{... | collective-permute-start | bytes 319496 | tf_op jit(solution)/shard_map/ppermute | solution.py:432

commit v2 on v1

--- a/solution.py
+++ b/solution.py
@@ -71,15 +71,14 @@
     return result
 
 
-def prepare_kernel(counts, offsets, lines, burgers, translation, out, after, before, alone):
+def prepare_kernel(counts, segments, out, after, before, alone):
     slot = lax.broadcasted_iota(jnp.int32, (cells, slots), 1)
     mask = (slot < by_cell(counts)).astype(f32)
-    place = [offsets[axis] for axis in range(3)]
-    line = [lines[axis] for axis in range(3)]
-    charge = [burgers[axis] * mask for axis in range(3)]
-    for axis in range(3):
-        out[axis] = place[axis]
-        out[3 + axis] = line[axis]
+    place = [segments[axis] for axis in range(3)]
+    line = [segments[3 + axis] for axis in range(3)]
+    charge = [segments[6 + axis] * mask for axis in range(3)]
+    out[0:6] = segments[0:6]
+    for axis in range(3):
         out[6 + axis] = charge[axis]
     strength = crossed(charge, line)
     poly = monomials(place)
@@ -89,9 +88,7 @@
             weighted = strength[axis] if value is None else value * strength[axis]
             total = jnp.sum(weighted, axis=1, keepdims=True)
             moments = jnp.where(slot == axis * len(poly) + term, total, moments)
-    moved = jnp.dot(
-        moments * (1.0 / slots), translation[...], precision=highest, preferred_element_type=f32
-    )
+    moved = moments * (1.0 / slots)
     out[9] = moved
     alone[...] = moved
     for plane, message in ((0, after), (1, before)):
@@ -200,12 +197,16 @@
     return place, [block[3 + axis] for axis in range(3)], [block[6 + axis] for axis in range(3)]
 
 
+def target_order():
+    return [4 * x + 2 * y + z for x in range(2) for z in range(2) for y in range(2)]
+
+
 def add_targets(block, base, targets, stage):
     for index, row in enumerate(target_rows(*moved_block(block, base))):
         stage[index * cells : (index + 1) * cells, :] = row
-    for cell in range(cells):
+    for position, cell in enumerate(target_order()):
         rows = stage[pl.ds(cell, features, stride=cells), :]
-        targets[cell * slots : (cell + 1) * slots, :] = rows.T.astype(bf16)
+        targets[position * slots : (position + 1) * slots, :] = rows.T.astype(bf16)
 
 
 def add_sources(block, base, columns, parts, positions, stage):
@@ -238,7 +239,7 @@
     return jnp.dot(mine, columns[:, pl.ds(start, count * width)], preferred_element_type=f32)
 
 
-def add_pairs(totals, value, parts, first, count, fresh):
+def add_pairs(before, after, row, value, parts, first, count):
     start = pl.multiple_of(first * 8, 8)
     sources = []
     for cell in range(count):
@@ -261,8 +262,8 @@
             terms.append(along)
             sums = [term if s is None else s + term for s, term in zip(sums, terms)]
         for index in range(4):
-            place = slice(index * slots + group * 8, index * slots + group * 8 + 8)
-            totals[place, :] = sums[index] if fresh else totals[place, :] + sums[index]
+            place = pl.ds(pl.multiple_of(row + index * cells * slots + group * 8, 8), 8)
+            after[place, :] = sums[index] if before is None else before[place, :] + sums[index]
 
 
 def own_cells():
@@ -298,89 +299,89 @@
     return result
 
 
-def near_sums(targets, groups, runs_of, earlier, columns, parts, stage, totals, mixed, gathered):
+def near_sums(targets, groups, tasks_of, before, after, columns, parts, stage):
     for block, places, positions in groups:
         add_sources(block, base_of(places), columns, parts, positions, stage)
 
-    def one_target(target, carry):
-        mine = targets[pl.ds(pl.multiple_of(target * slots, slots), slots), :]
-        runs = runs_of(target // 4, target // 2 % 2, target % 2)
-        value = pair_products(mine, columns, *runs[0])
-        for index, run in enumerate(runs):
-            later = None
-            if index + 1 < len(runs):
-                later = pair_products(mine, columns, *runs[index + 1])
-            add_pairs(totals, value, parts, *run, index == 0)
-            value = later
-        lane = lax.broadcasted_iota(jnp.int32, (slots, slots), 1)
-        for index in range(4):
-            total = jnp.sum(totals[index * slots : (index + 1) * slots, :], axis=1, keepdims=True)
-            mixed[...] = jnp.where(lane == index * cells + target, total, mixed[...])
+    def one_pair(pair, carry):
+        tasks = tasks_of(pair // 2, pair % 2)
+
+        def products(task):
+            row = pl.multiple_of((pair * 2 + task[0]) * slots, slots)
+            mine = targets[pl.ds(row, task[1] * slots), :]
+            return row, pair_products(mine, columns, *task[2:])
+
+        ready = products(tasks[0])
+        seen = set()
+        for index, task in enumerate(tasks):
+            later = products(tasks[index + 1]) if index + 1 < len(tasks) else None
+            earlier = after if task[0] in seen else before
+            seen.add(task[0])
+            add_pairs(earlier, after, *ready, parts, *task[2:])
+            ready = later
         return carry
 
-    mixed[...] = jnp.zeros((slots, slots), f32)
-    lax.fori_loop(0, cells, one_target, 0)
-    result = mixed[...].T[: 4 * cells, :]
-    gathered[...] = result if earlier is None else result + earlier[...]
+    lax.fori_loop(0, cells // 2, one_pair, 0)
 
 
 def rows_of(block, first=0):
     return [block[axis, first : first + cells, :] for axis in range(9)]
 
 
-def own_kernel(own, message, targets, out, *scratch):
+def own_kernel(own, message, targets, sums, *scratch):
     add_targets(rows_of(own), base_of(own_cells()), targets, scratch[2])
     groups = [(rows_of(own), own_cells(), list(range(8)))]
 
-    def runs(x, y, z):
-        return [(first, 2) for first in (0, 2, 4, 6)]
-
-    near_sums(targets, groups, runs, None, *scratch, out)
-
-
-def z_kernel(targets, halo, earlier, out, *scratch):
+    def tasks(x, z):
+        return [(0, 2, first, 2) for first in (0, 2, 4, 6)]
+
+    near_sums(targets, groups, tasks, None, sums, *scratch)
+
+
+def z_kernel(targets, halo, before, after, *scratch):
     groups = [(rows_of(halo, 8), z_cells(), list(range(8)))]
 
-    def runs(x, y, z):
-        return [(4 * (1 - z) + first, 2) for first in (0, 2)]
-
-    near_sums(targets, groups, runs, earlier, *scratch, out)
-
-
-def x_kernel(targets, halo, message, earlier, out, *scratch):
+    def tasks(x, z):
+        return [(0, 2, 4 * (1 - z) + first, 2) for first in (0, 2)]
+
+    near_sums(targets, groups, tasks, before, after, *scratch)
+
+
+def x_kernel(targets, halo, message, before, after, *scratch):
     groups = []
     for index, places in enumerate(x_cells()):
         positions = [(0 if x == 3 else 8) + 2 * z + y - 1 for x, y, z in places]
         groups.append((rows_of(halo, 8 * index), places, positions))
 
-    def runs(x, y, z):
-        return [(8 * (1 - x) + 2 * z + first, 2) for first in (0, 2, 4)]
-
-    near_sums(targets, groups, runs, earlier, *scratch, out)
+    def tasks(x, z):
+        return [(0, 2, 8 * (1 - x) + 2 * z + first, 2) for first in (0, 2, 4)]
+
+    near_sums(targets, groups, tasks, before, after, *scratch)
 
 
 def y_kernel(
-    starts, stress, mobility, counts, own, targets, high, low, earlier, weights_far, *rest
+    starts, stress, mobility, counts, own, targets, high, low, before, weights_far, translation, *rest
 ):
     tails, out, scratch = (rest[: len(starts)], rest[len(starts)], rest[len(starts) + 1 :])
-    gathered = scratch[-1]
+    after = scratch[-1]
     groups = []
     for block, side in ((high, 3), (low, 0)):
         for index, places in enumerate(y_cells(side)):
             positions = [(16 if side else 0) + 4 * x + z for x, y, z in places]
             groups.append((rows_of(block, 8 * index), places, positions))
 
-    def runs(x, y, z):
-        return [(16 * y + 4 * (x + line) + z, 3) for line in range(3)]
-
-    near_sums(targets, groups, runs, earlier, *scratch)
-    sums_of = [gathered[index * cells : (index + 1) * cells, :] for index in range(4)]
+    def tasks(x, z):
+        return [(y, 1, 16 * y + 4 * (x + line) + z, 3) for y in range(2) for line in range(3)]
+
     local = [tail[index] for start, tail in zip(starts, tails) for index in range(start, tail.shape[0])]
     coefficients = jnp.dot(
         weights_far[...],
         jnp.concatenate(local, axis=0),
         precision=highest,
         preferred_element_type=f32,
+    )
+    coefficients = jnp.dot(
+        coefficients, translation[...], precision=highest, preferred_element_type=f32
     )
     place = [own[axis] for axis in range(3)]
     line = [own[3 + axis] for axis in range(3)]
@@ -393,18 +394,31 @@
         for a in range(3)
     ]
     applied = crossed(stressed, line)
-    force = []
-    for axis in range(3):
-        at = place[axis] + base[axis]
-        near = sums_of[axis] - at * sums_of[3]
+    outside = []
+    for axis in range(3):
         far = jnp.zeros((cells, slots), f32)
         for term, value in enumerate(poly):
             column = axis * len(poly) + term
             coefficient = coefficients[:, column : column + 1]
             far = far + (coefficient if value is None else coefficient * value)
-        force.append(near_scale * near + far * mask + applied[axis])
+        outside.append(far * mask + applied[axis])
+    scale = by_cell(mobility) * mask
+    near_sums(targets, groups, tasks, before, after, *scratch[:-1])
+    lane = lax.broadcasted_iota(jnp.int32, (slots, slots), 1)
+    mixed = jnp.zeros((slots, slots), f32)
+    for position, cell in enumerate(target_order()):
+        for index in range(4):
+            first = (index * cells + position) * slots
+            total = jnp.sum(after[first : first + slots, :], axis=1, keepdims=True)
+            mixed = jnp.where(lane == index * cells + cell, total, mixed)
+    mixed = mixed.T
+    sums_of = [mixed[index * cells : (index + 1) * cells, :] for index in range(4)]
+    force = []
+    for axis in range(3):
+        at = place[axis] + base[axis]
+        near = sums_of[axis] - at * sums_of[3]
+        force.append(near_scale * near + outside[axis])
     ratio = dotted(force, line) / jnp.maximum(dotted(line, line), 1.0)
-    scale = by_cell(mobility) * mask
     for axis in range(3):
         out[axis] = scale * (force[axis] - ratio * line[axis])
 
@@ -439,11 +453,9 @@
         pltpu.VMEM((features, count * forms * slots), bf16),
         pltpu.VMEM((count * 8, slots), f32),
         pltpu.VMEM((features * cells, slots), f32),
-        pltpu.VMEM((4 * slots, slots), f32),
-        pltpu.VMEM((slots, slots), f32),
     ]
     if last:
-        scratch.append(pltpu.VMEM((4 * cells, slots), f32))
+        scratch.append(pltpu.VMEM((4 * cells * slots, slots), f32))
     return pl.pallas_call(
         kernel,
         out_shape=shape,
@@ -460,7 +472,7 @@
 
 def body(offsets, lines, burgers, counts, mobility, stress, translation):
     sizes = [lax.axis_size(axis) for axis in ("gx", "gy", "gz")]
-    flat = [value.reshape(3, cells, slots) for value in (offsets, lines, burgers)]
+    segments = jnp.concatenate([offsets, lines, burgers], axis=0).reshape(9, cells, slots)
     vmem = pl.BlockSpec(memory_space=pltpu.VMEM)
     smem = pl.BlockSpec(memory_space=pltpu.SMEM)
     message = jax.ShapeDtypeStruct((11, 4, slots), f32)
@@ -468,15 +480,15 @@
     own, up, down, moments = pl.pallas_call(
         prepare_kernel,
         out_shape=(block, message, message, jax.ShapeDtypeStruct((cells, slots), f32)),
-        in_specs=[smem] + [vmem] * 4,
+        in_specs=[smem, vmem],
         out_specs=(vmem,) * 4,
         compiler_params=pltpu.CompilerParams(vmem_limit_bytes=4 * 1024 * 1024),
         name="prepare",
-    )(counts, *flat, translation)
+    )(counts, segments)
     high = shifted(up, "gz", 1)
     low = shifted(down, "gz", -1)
     middle = [shifted(moments, "gz", step) for step in range(2, sizes[2] - 1)]
-    sums = jax.ShapeDtypeStruct((4 * cells, slots), f32)
+    sums = jax.ShapeDtypeStruct((4 * cells * slots, slots), f32)
     both = (jax.ShapeDtypeStruct((cells * slots, features), bf16), sums)
     targets, partial = near_call(own_kernel, "near_own", 8, 64, [], [own, up], both)
     message = pl.pallas_call(
@@ -535,7 +547,7 @@
         32,
         72,
         [stress, mobility, counts],
-        [own, targets, high, low, partial, jnp.asarray(far_weights(sizes))] + tails,
+        [own, targets, high, low, partial, jnp.asarray(far_weights(sizes)), translation] + tails,
         jax.ShapeDtypeStruct((3, cells, slots), f32),
         last=True,
     )

time: 38.7 us -> 33.5 us (0.87)
  Pallas kernels: 21.7 us -> 18 us
  local copies, waits for them, and re-layouts: 3.65 us -> 0.7 us
  other arithmetic: 0 us -> 0.76 us
  waiting for transfers between devices: 0.02 us -> 0.74 us
    pallas_call x4, Pallas kernels: 20.7 us -> 17.1 us  [near_call(): pl.pallas_call(kernel, out_shape=shape, in_specs=[smem] * len(scalars) +...]
    unnamed x16 -> x12, local copies, waits for them, and re-layouts: 3.65 us -> 0.7 us
    concatenate x0 -> x1, other arithmetic: none -> 0.76 us  [body(): jnp.concatenate([offsets, lines, burgers], axis=0).reshape(9, cells, slots)]
    ppermute x7, waiting for transfers between devices: 0.02 us -> 0.74 us  [shifted(): lax.ppermute(value, axis, [(i, (i - step) % count) for i in range(count)])]
  transfers between devices with their start and end apart: 7 -> 7, of which waited for: 0 -> 1; matrix products, arithmetic and copies ran while one was open for 0% -> 0% of each run, Pallas kernels for 34% -> 29%
where the time goes in v2:
time: 33.5 us; the launch traced here: 33.2 us
  Pallas kernels  18 us (54%)
  starting transfers between devices  12.8 us (38%)
  other arithmetic  0.76 us (2%)
  waiting for transfers between devices  0.74 us (2%)
  local copies, waits for them, and re-layouts  0.7 us (2%)
    pallas_call x4, Pallas kernels, near_call(): pl.pallas_call(kernel, out_shape=shape, in_specs=[smem] * len(scalars) +...  17.1 us
    ppermute x7, starting transfers between devices, shifted(): lax.ppermute(value, axis, [(i, (i - step) % count) for i in range(count)])  12.8 us
    pallas_call x1, Pallas kernels, body(): pl.pallas_call(prepare_kernel, out_shape=(block, message, message, jax.Sh...  0.76 us
    concatenate x1, other arithmetic, body(): jnp.concatenate([offsets, lines, burgers], axis=0).reshape(9, cells, slots)  0.76 us
    ppermute x7, waiting for transfers between devices, shifted(): lax.ppermute(value, axis, [(i, (i - step) % count) for i in range(count)])  0.74 us
    unnamed x12, local copies, waits for them, and re-layouts  0.7 us
  transfers between devices with their start and end apart: 7, of which 1 were waited for; matrix products, arithmetic and copies ran while one was open for 0% of the time, Pallas kernels for 29%

profile of v2, /device:TPU:0, one launch (start us, length us, event | category | flops | bytes accessed | tf_op | source)
XLA Modules:
  0.0 33.2 jit_solution(2784830852751667424)
XLA Ops:
  0.0 0.8 %pad_maximum_fusion = f32[9,2,2,2,128]{4,3,2,1,0:T(2,128)S(1)} fusion(f32[3,2,2,2,128]{4,3,2,1,0:T(2,128)} %param.10, f32[3,2,2,2,128]{4,3,2,1,0:T(2,128)} %param.9, f32[3,2,2,2,128]{4,3,2,1,0:T(2,128)} %param.8), kind=kLoop, calls=%fused_computation | loop fusion | flops 18432 | bytes 73728 | tf_op jit(solution)/shard_map/concatenate | solution.py:475
  0.8 0.0 copy-start
  0.8 0.7 %copy-done = s32[2,2,2]{2,1,0:T(2,128)S(1)} copy-done((s32[2,2,2]{2,1,0:T(2,128)S(1)}, s32[2,2,2]{2,1,0:T(2,128)}, u32[]{:S(2)}) %copy-start) | copy-done | bytes 56
  1.4 0.8 %prepare.1 = (f32[10,8,128]{2,1,0:T(8,128)S(1)}, f32[11,4,128]{2,1,0:T(4,128)S(1)}, f32[11,4,128]{2,1,0:T(4,128)S(1)}, f32[8,128]{1,0:T(8,128)S(1)}) custom-call(s32[2,2,2]{2,1,0:T(2,128)S(1)} %copy-done, f32[9,8,128]{2,1,0:T(8,128)S(1)} %bitcast.2), custom_call_target="tpu_custom_call" | custom-call | tf_op jit(solution)/shard_map/prepare/pallas_call | solution.py:480
  2.2 4.1 %collective-permute-start.2 = (f32[8,128]{1,0:T(8,128)S(1)}, f32[8,128]{1,0:T(8,128)S(1)}, u32[]{:S(2)}, u32[]{:S(2)}) collective-permute-start(f32[8,128]{1,0:T(8,128)S(1)} %get-tuple-element.18), channel_id=1, source_target_pairs={{0,2},{1,3},{2,0},{3,1},{4,6},{5,7},{6,4},{7,5},{8,10},{9,11},{10,... | collective-permute-start | bytes 12296 | tf_op jit(solution)/shard_map/ppermute | solution.py:446
  6.3 1.6 %collective-permute-start.1 = (f32[11,4,128]{2,1,0:T(4,128)S(1)}, f32[11,4,128]{2,1,0:T(4,128)S(1)}, u32[]{:S(2)}, u32[]{:S(2)}) collective-permute-start(f32[11,4,128]{2,1,0:T(4,128)S(1)} %get-tuple-element.17), channel_id=1, source_target_pairs={{0,1},{1,2},{2,3},{3,0},{4,5},{5,6},{6,7},{7,4},{8,9},{9,10},{10,1... | collective-permute-start | bytes 67592 | tf_op jit(solution)/shard_map/ppermute | solution.py:446
  7.9 2.2 %collective-permute-start = (f32[11,4,128]{2,1,0:T(4,128)S(1)}, f32[11,4,128]{2,1,0:T(4,128)S(1)}, u32[]{:S(2)}, u32[]{:S(2)}) collective-permute-start(f32[11,4,128]{2,1,0:T(4,128)S(1)} %get-tuple-element.15.message), channel_id=1, source_target_pairs={{0,3},{1,0},{2,1},{3,2},{4,7},{5,4},{6,5},{7,6},{8,11},{9,8},{10,9... | collective-permute-start | bytes 67592 | tf_op jit(solution)/shard_map/ppermute | solution.py:446
  10.1 4.2 %near_own.1 = (bf16[1024,64]{1,0:T(8,128)(2,1)S(1)}, f32[4096,128]{1,0:T(8,128)S(1)}) custom-call(f32[10,8,128]{2,1,0:T(8,128)S(1)} %get-tuple-element.14.own, f32[11,4,128]{2,1,0:T(4,128)S(1)} %get-tuple-element.15.message), custom_call_target="tpu_custom_call" | custom-call | flops 8388608000 | bytes 1048576 | tf_op jit(solution)/shard_map/near_own/pallas_call | solution.py:459
  14.3 0.0 collective-permute-done.2.rest_0_
  14.3 0.0 collective-permute-done.1.low
  14.3 0.0 collective-permute-done.high
  14.4 1.6 %collective-permute-start.3 = (f32[11,16,128]{2,1,0:T(8,128)S(1)}, f32[11,16,128]{2,1,0:T(8,128)S(1)}, u32[]{:S(2)}, u32[]{:S(2)}) collective-permute-start(f32[11,16,128]{2,1,0:T(8,128)S(1)} %pack_x.1.halo.inner.rest_0_), channel_id=1, source_target_pairs={{0,16},{16,0},{1,17},{17,1},{2,18},{18,2},{3,19},{19,3},{4,20},{20... | collective-permute-start | bytes 270344 | tf_op jit(solution)/shard_map/ppermute | solution.py:446
  15.9 2.3 %near_z.1.rest_2_.before = f32[4096,128]{1,0:T(8,128)S(1)} custom-call(bf16[1024,64]{1,0:T(8,128)(2,1)S(1)} %get-tuple-element.16.targets, f32[11,16,128]{2,1,0:T(8,128)S(1)} %pack_x.1.halo.inner.rest_0_, f32[4096,128]{1,0:T(8,128)S(1)} %get-tuple-element.19.rest_1_.before), custom_call_target="tpu_custom_call" | custom-call | flops 4194304000 | bytes 1048576 | tf_op jit(solution)/shard_map/near_z/pallas_call | solution.py:459
  18.2 0.7 %collective-permute-done.3.outer.rest_1_.halo = f32[11,16,128]{2,1,0:T(8,128)S(1)} collective-permute-done((f32[11,16,128]{2,1,0:T(8,128)S(1)}, f32[11,16,128]{2,1,0:T(8,128)S(1)}, u32[]{:S(2)}, u32[]{:S(2)}) %collective-permute-start.3) | collective-permute-done | bytes 90144 | tf_op jit(solution)/shard_map/ppermute | solution.py:446
  19.0 0.1 pack_y.1
  19.0 1.6 %collective-permute-start.6 = (f32[4,16,128]{2,1,0:T(8,128)S(1)}, f32[4,16,128]{2,1,0:T(8,128)S(1)}, u32[]{:S(2)}, u32[]{:S(2)}) collective-permute-start(f32[4,16,128]{2,1,0:T(8,128)S(1)} %get-tuple-element.22), channel_id=1, source_target_pairs={{0,8},{4,12},{8,0},{12,4},{1,9},{5,13},{9,1},{13,5},{2,10},{6,14},... | collective-permute-start | bytes 98312 | tf_op jit(solution)/shard_map/ppermute | solution.py:446
  20.6 0.0 collective-permute-start.5
  20.6 0.0 copy-start.4
  20.6 0.0 copy-start.5
  20.6 1.8 %collective-permute-start.4 = (f32[13,16,128]{2,1,0:T(8,128)S(1)}, f32[13,16,128]{2,1,0:T(8,128)S(1)}, u32[]{:S(2)}, u32[]{:S(2)}) collective-permute-start(f32[13,16,128]{2,1,0:T(8,128)S(1)} %get-tuple-element.20.message), channel_id=1, source_target_pairs={{0,12},{4,0},{8,4},{12,8},{1,13},{5,1},{9,5},{13,9},{2,14},{6,2},{... | collective-permute-start | bytes 319496 | tf_op jit(solution)/shard_map/ppermute | solution.py:446
  22.4 3.3 %near_x.1.before = f32[4096,128]{1,0:T(8,128)S(1)} custom-call(bf16[1024,64]{1,0:T(8,128)(2,1)S(1)} %get-tuple-element.16.targets, f32[11,16,128]{2,1,0:T(8,128)S(1)} %collective-permute-done.3.outer.rest_1_.halo, f32[13,16,128]{2,1,0:T(8,128)S(1)} %get-tuple-element.20.message, f32[4096,128]{1,0:T(8,128)S(1)} %near_z.1.rest_2_.before), custom_call_target="tpu_custom_call" | custom-call | flops 6291456000 | bytes 1048576 | tf_op jit(solution)/shard_map/near_x/pallas_call | solution.py:459
  25.7 0.0 collective-permute-done.6.rest_3_
  25.7 0.0 collective-permute-done.5.low.rest_4_
  25.8 7.4 %near_y.1 = f32[3,8,128]{2,1,0:T(8,128)} custom-call(f32[3,3]{1,0:T(4,128)S(1)} %copy-done.3, f32[2,2,2]{2,1,0:T(2,128)S(1)} %copy-done.4, s32[2,2,2]{2,1,0:T(2,128)S(1)} %copy-done.1, f32[10,8,128]{2,1,0:T(8,128)S(1)} %get-tuple-element.14.own, bf16[1024,64]{1,0:T(8,128)(2,1)S(1)} %get-tuple-element.16.targets, ...), custom_call_target="tpu_custom_call" | custom-call | flops 9437184000 | bytes 1048576 | tf_op jit(solution)/shard_map/near_y/pallas_call | solution.py:459
  (10 shorter events, 0.0 us)
Async XLA Ops:
  0.8 0.7 %copy-start = (s32[2,2,2]{2,1,0:T(2,128)S(1)}, s32[2,2,2]{2,1,0:T(2,128)}, u32[]{:S(2)}) copy-start(s32[2,2,2]{2,1,0:T(2,128)} %counts.3) | copy-start | bytes 100
  2.2 12.1 %collective-permute-start.2 = (f32[8,128]{1,0:T(8,128)S(1)}, f32[8,128]{1,0:T(8,128)S(1)}, u32[]{:S(2)}, u32[]{:S(2)}) collective-permute-start(f32[8,128]{1,0:T(8,128)S(1)} %get-tuple-element.18), channel_id=1, source_target_pairs={{0,2},{1,3},{2,0},{3,1},{4,6},{5,7},{6,4},{7,5},{8,10},{9,11},{10,... | collective-permute-start | bytes 12296 | tf_op jit(solution)/shard_map/ppermute | solution.py:446
  6.3 8.0 %collective-permute-start.1 = (f32[11,4,128]{2,1,0:T(4,128)S(1)}, f32[11,4,128]{2,1,0:T(4,128)S(1)}, u32[]{:S(2)}, u32[]{:S(2)}) collective-permute-start(f32[11,4,128]{2,1,0:T(4,128)S(1)} %get-tuple-element.17), channel_id=1, source_target_pairs={{0,1},{1,2},{2,3},{3,0},{4,5},{5,6},{6,7},{7,4},{8,9},{9,10},{10,1... | collective-permute-start | bytes 67592 | tf_op jit(solution)/shard_map/ppermute | solution.py:446
  7.9 6.4 %collective-permute-start = (f32[11,4,128]{2,1,0:T(4,128)S(1)}, f32[11,4,128]{2,1,0:T(4,128)S(1)}, u32[]{:S(2)}, u32[]{:S(2)}) collective-permute-start(f32[11,4,128]{2,1,0:T(4,128)S(1)} %get-tuple-element.15.message), channel_id=1, source_target_pairs={{0,3},{1,0},{2,1},{3,2},{4,7},{5,4},{6,5},{7,6},{8,11},{9,8},{10,9... | collective-permute-start | bytes 67592 | tf_op jit(solution)/shard_map/ppermute | solution.py:446
  14.4 4.6 %collective-permute-start.3 = (f32[11,16,128]{2,1,0:T(8,128)S(1)}, f32[11,16,128]{2,1,0:T(8,128)S(1)}, u32[]{:S(2)}, u32[]{:S(2)}) collective-permute-start(f32[11,16,128]{2,1,0:T(8,128)S(1)} %pack_x.1.halo.inner.rest_0_), channel_id=1, source_target_pairs={{0,16},{16,0},{1,17},{17,1},{2,18},{18,2},{3,19},{19,3},{4,20},{20... | collective-permute-start | bytes 270344 | tf_op jit(solution)/shard_map/ppermute | solution.py:446
  19.0 6.7 %collective-permute-start.6 = (f32[4,16,128]{2,1,0:T(8,128)S(1)}, f32[4,16,128]{2,1,0:T(8,128)S(1)}, u32[]{:S(2)}, u32[]{:S(2)}) collective-permute-start(f32[4,16,128]{2,1,0:T(8,128)S(1)} %get-tuple-element.22), channel_id=1, source_target_pairs={{0,8},{4,12},{8,0},{12,4},{1,9},{5,13},{9,1},{13,5},{2,10},{6,14},... | collective-permute-start | bytes 98312 | tf_op jit(solution)/shard_map/ppermute | solution.py:446
  20.6 5.1 %collective-permute-start.5 = (f32[13,16,128]{2,1,0:T(8,128)S(1)}, f32[13,16,128]{2,1,0:T(8,128)S(1)}, u32[]{:S(2)}, u32[]{:S(2)}) collective-permute-start(f32[13,16,128]{2,1,0:T(8,128)S(1)} %get-tuple-element.21), channel_id=1, source_target_pairs={{0,4},{4,8},{8,12},{12,0},{1,5},{5,9},{9,13},{13,1},{2,6},{6,10},{... | collective-permute-start | bytes 319496 | tf_op jit(solution)/shard_map/ppermute | solution.py:446
  20.6 5.2 %copy-start.1 = (s32[2,2,2]{2,1,0:T(2,128)S(1)}, s32[2,2,2]{2,1,0:T(2,128)}, u32[]{:S(2)}) copy-start(s32[2,2,2]{2,1,0:T(2,128)} %counts.3) | copy-start | bytes 100
  20.6 5.2 %copy-start.2 = (f32[128,128]{1,0:T(8,128)S(1)}, f32[128,128]{1,0:T(8,128)}, u32[]{:S(2)}) copy-start(f32[128,128]{1,0:T(8,128)} %translation.1) | copy-start | bytes 196612
  20.6 5.2 %copy-start.3 = (f32[3,3]{1,0:T(4,128)S(1)}, f32[3,3]{1,0:T(4,128)}, u32[]{:S(2)}) copy-start(f32[3,3]{1,0:T(4,128)} %stress.1) | copy-start | bytes 112
  20.6 5.2 %copy-start.4 = (f32[2,2,2]{2,1,0:T(2,128)S(1)}, f32[2,2,2]{2,1,0:T(2,128)}, u32[]{:S(2)}) copy-start(f32[2,2,2]{2,1,0:T(2,128)} %mobility.1) | copy-start | bytes 100
  20.6 5.2 %copy-start.5 = (f32[8,256]{1,0:T(8,128)S(1)}, f32[8,256]{1,0:T(8,128)}, u32[]{:S(2)}) copy-start(f32[8,256]{1,0:T(8,128)} %constant.2.clone.weights_far) | copy-start | bytes 24580
  20.6 5.1 %collective-permute-start.4 = (f32[13,16,128]{2,1,0:T(8,128)S(1)}, f32[13,16,128]{2,1,0:T(8,128)S(1)}, u32[]{:S(2)}, u32[]{:S(2)}) collective-permute-start(f32[13,16,128]{2,1,0:T(8,128)S(1)} %get-tuple-element.20.message), channel_id=1, source_target_pairs={{0,12},{4,0},{8,4},{12,8},{1,13},{5,1},{9,5},{13,9},{2,14},{6,2},{... | collective-permute-start | bytes 319496 | tf_op jit(solution)/shard_map/ppermute | solution.py:446

commit v3 on v2

--- a/solution.py
+++ b/solution.py
@@ -299,29 +299,37 @@
     return result
 
 
-def near_sums(targets, groups, tasks_of, before, after, columns, parts, stage):
+def near_sums(
+    targets, groups, tasks_of, before, after, columns, parts, stage, unroll=2, finish=None
+):
     for block, places, positions in groups:
         add_sources(block, base_of(places), columns, parts, positions, stage)
 
-    def one_pair(pair, carry):
-        tasks = tasks_of(pair // 2, pair % 2)
-
-        def products(task):
+    def several_pairs(step, carry):
+        tasks = []
+        for index in range(unroll):
+            pair = step * unroll + index
+            tasks += [(index, pair, task) for task in tasks_of(pair // 2, pair % 2)]
+
+        def products(index, pair, task):
             row = pl.multiple_of((pair * 2 + task[0]) * slots, slots)
             mine = targets[pl.ds(row, task[1] * slots), :]
             return row, pair_products(mine, columns, *task[2:])
 
-        ready = products(tasks[0])
-        seen = set()
-        for index, task in enumerate(tasks):
-            later = products(tasks[index + 1]) if index + 1 < len(tasks) else None
-            earlier = after if task[0] in seen else before
-            seen.add(task[0])
-            add_pairs(earlier, after, *ready, parts, *task[2:])
+        ready = products(*tasks[0])
+        seen = None
+        for order, (index, pair, task) in enumerate(tasks):
+            following = tasks[order + 1] if order + 1 < len(tasks) else None
+            later = products(*following) if following else None
+            now = (index, task[0])
+            add_pairs(after if now == seen else before, after, *ready, parts, *task[2:])
+            seen = now
+            if finish and (following is None or (following[0], following[2][0]) != now):
+                finish(pair * 2 + task[0], pair // 2 * 4 + pair % 2 + 2 * task[0])
             ready = later
         return carry
 
-    lax.fori_loop(0, cells // 2, one_pair, 0)
+    lax.fori_loop(0, cells // 2 // unroll, several_pairs, 0)
 
 
 def rows_of(block, first=0):
@@ -344,7 +352,7 @@
     def tasks(x, z):
         return [(0, 2, 4 * (1 - z) + first, 2) for first in (0, 2)]
 
-    near_sums(targets, groups, tasks, before, after, *scratch)
+    near_sums(targets, groups, tasks, before, after, *scratch, unroll=4)
 
 
 def x_kernel(targets, halo, message, before, after, *scratch):
@@ -363,7 +371,7 @@
     starts, stress, mobility, counts, own, targets, high, low, before, weights_far, translation, *rest
 ):
     tails, out, scratch = (rest[: len(starts)], rest[len(starts)], rest[len(starts) + 1 :])
-    after = scratch[-1]
+    after, gathered = scratch[-2:]
     groups = []
     for block, side in ((high, 3), (low, 0)):
         for index, places in enumerate(y_cells(side)):
@@ -403,15 +411,17 @@
             far = far + (coefficient if value is None else coefficient * value)
         outside.append(far * mask + applied[axis])
     scale = by_cell(mobility) * mask
-    near_sums(targets, groups, tasks, before, after, *scratch[:-1])
     lane = lax.broadcasted_iota(jnp.int32, (slots, slots), 1)
-    mixed = jnp.zeros((slots, slots), f32)
-    for position, cell in enumerate(target_order()):
+
+    def finish(position, cell):
         for index in range(4):
-            first = (index * cells + position) * slots
-            total = jnp.sum(after[first : first + slots, :], axis=1, keepdims=True)
-            mixed = jnp.where(lane == index * cells + cell, total, mixed)
-    mixed = mixed.T
+            first = pl.multiple_of((index * cells + position) * slots, slots)
+            total = jnp.sum(after[pl.ds(first, slots), :], axis=1, keepdims=True)
+            gathered[...] = jnp.where(lane == index * cells + cell, total, gathered[...])
+
+    gathered[...] = jnp.zeros((slots, slots), f32)
+    near_sums(targets, groups, tasks, before, after, *scratch[:-2], finish=finish)
+    mixed = gathered[...].T
     sums_of = [mixed[index * cells : (index + 1) * cells, :] for index in range(4)]
     force = []
     for axis in range(3):
@@ -456,6 +466,7 @@
     ]
     if last:
         scratch.append(pltpu.VMEM((4 * cells * slots, slots), f32))
+        scratch.append(pltpu.VMEM((slots, slots), f32))
     return pl.pallas_call(
         kernel,
         out_shape=shape,

time: 33.5 us -> 32.8 us (0.979)
  Pallas kernels: 18 us -> 17 us
    pallas_call x4, Pallas kernels: 17.1 us -> 16.2 us  [near_call(): pl.pallas_call(kernel, out_shape=shape, in_specs=[smem] * len(scalars) +...]
  transfers between devices with their start and end apart: 7 -> 7, of which waited for: 1 -> 1; matrix products, arithmetic and copies ran while one was open for 0% -> 0% of each run, Pallas kernels for 29% -> 28%
where the time goes in v3:
time: 32.8 us; the launch traced here: 32.5 us
  Pallas kernels  17 us (52%)
  starting transfers between devices  12.8 us (39%)
  waiting for transfers between devices  0.95 us (3%)
  other arithmetic  0.76 us (2%)
  local copies, waits for them, and re-layouts  0.7 us (2%)
    pallas_call x4, Pallas kernels, near_call(): pl.pallas_call(kernel, out_shape=shape, in_specs=[smem] * len(scalars) +...  16.2 us
    ppermute x7, starting transfers between devices, shifted(): lax.ppermute(value, axis, [(i, (i - step) % count) for i in range(count)])  12.8 us
    ppermute x7, waiting for transfers between devices, shifted(): lax.ppermute(value, axis, [(i, (i - step) % count) for i in range(count)])  0.95 us
    pallas_call x1, Pallas kernels, body(): pl.pallas_call(prepare_kernel, out_shape=(block, message, message, jax.Sh...  0.76 us
    concatenate x1, other arithmetic, body(): jnp.concatenate([offsets, lines, burgers], axis=0).reshape(9, cells, slots)  0.76 us
    unnamed x12, local copies, waits for them, and re-layouts  0.7 us
  transfers between devices with their start and end apart: 7, of which 1 were waited for; matrix products, arithmetic and copies ran while one was open for 0% of the time, Pallas kernels for 28%

profile of v3, /device:TPU:0, one launch (start us, length us, event | category | flops | bytes accessed | tf_op | source)
XLA Modules:
  0.0 32.5 jit_solution(7897549766445066488)
XLA Ops:
  0.0 0.8 %pad_maximum_fusion = f32[9,2,2,2,128]{4,3,2,1,0:T(2,128)S(1)} fusion(f32[3,2,2,2,128]{4,3,2,1,0:T(2,128)} %param.10, f32[3,2,2,2,128]{4,3,2,1,0:T(2,128)} %param.9, f32[3,2,2,2,128]{4,3,2,1,0:T(2,128)} %param.8), kind=kLoop, calls=%fused_computation | loop fusion | flops 18432 | bytes 73728 | tf_op jit(solution)/shard_map/concatenate | solution.py:486
  0.8 0.0 copy-start
  0.8 0.7 %copy-done = s32[2,2,2]{2,1,0:T(2,128)S(1)} copy-done((s32[2,2,2]{2,1,0:T(2,128)S(1)}, s32[2,2,2]{2,1,0:T(2,128)}, u32[]{:S(2)}) %copy-start) | copy-done | bytes 56
  1.4 0.8 %prepare.1 = (f32[10,8,128]{2,1,0:T(8,128)S(1)}, f32[11,4,128]{2,1,0:T(4,128)S(1)}, f32[11,4,128]{2,1,0:T(4,128)S(1)}, f32[8,128]{1,0:T(8,128)S(1)}) custom-call(s32[2,2,2]{2,1,0:T(2,128)S(1)} %copy-done, f32[9,8,128]{2,1,0:T(8,128)S(1)} %bitcast.2), custom_call_target="tpu_custom_call" | custom-call | tf_op jit(solution)/shard_map/prepare/pallas_call | solution.py:491
  2.2 4.1 %collective-permute-start.2 = (f32[8,128]{1,0:T(8,128)S(1)}, f32[8,128]{1,0:T(8,128)S(1)}, u32[]{:S(2)}, u32[]{:S(2)}) collective-permute-start(f32[8,128]{1,0:T(8,128)S(1)} %get-tuple-element.18), channel_id=1, source_target_pairs={{0,2},{1,3},{2,0},{3,1},{4,6},{5,7},{6,4},{7,5},{8,10},{9,11},{10,... | collective-permute-start | bytes 12296 | tf_op jit(solution)/shard_map/ppermute | solution.py:456
  6.3 1.6 %collective-permute-start.1 = (f32[11,4,128]{2,1,0:T(4,128)S(1)}, f32[11,4,128]{2,1,0:T(4,128)S(1)}, u32[]{:S(2)}, u32[]{:S(2)}) collective-permute-start(f32[11,4,128]{2,1,0:T(4,128)S(1)} %get-tuple-element.17), channel_id=1, source_target_pairs={{0,1},{1,2},{2,3},{3,0},{4,5},{5,6},{6,7},{7,4},{8,9},{9,10},{10,1... | collective-permute-start | bytes 67592 | tf_op jit(solution)/shard_map/ppermute | solution.py:456
  7.9 2.2 %collective-permute-start = (f32[11,4,128]{2,1,0:T(4,128)S(1)}, f32[11,4,128]{2,1,0:T(4,128)S(1)}, u32[]{:S(2)}, u32[]{:S(2)}) collective-permute-start(f32[11,4,128]{2,1,0:T(4,128)S(1)} %get-tuple-element.15.message), channel_id=1, source_target_pairs={{0,3},{1,0},{2,1},{3,2},{4,7},{5,4},{6,5},{7,6},{8,11},{9,8},{10,9... | collective-permute-start | bytes 67592 | tf_op jit(solution)/shard_map/ppermute | solution.py:456
  10.1 4.0 %near_own.1 = (bf16[1024,64]{1,0:T(8,128)(2,1)S(1)}, f32[4096,128]{1,0:T(8,128)S(1)}) custom-call(f32[10,8,128]{2,1,0:T(8,128)S(1)} %get-tuple-element.14.own, f32[11,4,128]{2,1,0:T(4,128)S(1)} %get-tuple-element.15.message), custom_call_target="tpu_custom_call" | custom-call | flops 8388608000 | bytes 1048576 | tf_op jit(solution)/shard_map/near_own/pallas_call | solution.py:470
  14.1 0.0 collective-permute-done.2.rest_0_
  14.2 0.0 collective-permute-done.1.low
  14.2 0.0 collective-permute-done.high
  14.2 1.6 %collective-permute-start.3 = (f32[11,16,128]{2,1,0:T(8,128)S(1)}, f32[11,16,128]{2,1,0:T(8,128)S(1)}, u32[]{:S(2)}, u32[]{:S(2)}) collective-permute-start(f32[11,16,128]{2,1,0:T(8,128)S(1)} %pack_x.1.halo.inner.rest_0_), channel_id=1, source_target_pairs={{0,16},{16,0},{1,17},{17,1},{2,18},{18,2},{3,19},{19,3},{4,20},{20... | collective-permute-start | bytes 270344 | tf_op jit(solution)/shard_map/ppermute | solution.py:456
  15.8 2.1 %near_z.1.rest_2_.before = f32[4096,128]{1,0:T(8,128)S(1)} custom-call(bf16[1024,64]{1,0:T(8,128)(2,1)S(1)} %get-tuple-element.16.targets, f32[11,16,128]{2,1,0:T(8,128)S(1)} %pack_x.1.halo.inner.rest_0_, f32[4096,128]{1,0:T(8,128)S(1)} %get-tuple-element.19.rest_1_.before), custom_call_target="tpu_custom_call" | custom-call | flops 4194304000 | bytes 1048576 | tf_op jit(solution)/shard_map/near_z/pallas_call | solution.py:470
  17.9 0.9 %collective-permute-done.3.outer.rest_1_.halo = f32[11,16,128]{2,1,0:T(8,128)S(1)} collective-permute-done((f32[11,16,128]{2,1,0:T(8,128)S(1)}, f32[11,16,128]{2,1,0:T(8,128)S(1)}, u32[]{:S(2)}, u32[]{:S(2)}) %collective-permute-start.3) | collective-permute-done | bytes 90144 | tf_op jit(solution)/shard_map/ppermute | solution.py:456
  18.8 0.1 pack_y.1
  18.9 1.6 %collective-permute-start.6 = (f32[4,16,128]{2,1,0:T(8,128)S(1)}, f32[4,16,128]{2,1,0:T(8,128)S(1)}, u32[]{:S(2)}, u32[]{:S(2)}) collective-permute-start(f32[4,16,128]{2,1,0:T(8,128)S(1)} %get-tuple-element.22), channel_id=1, source_target_pairs={{0,8},{4,12},{8,0},{12,4},{1,9},{5,13},{9,1},{13,5},{2,10},{6,14},... | collective-permute-start | bytes 98312 | tf_op jit(solution)/shard_map/ppermute | solution.py:456
  20.4 0.0 collective-permute-start.5
  20.4 0.0 copy-start.4
  20.5 0.0 copy-start.5
  20.5 1.8 %collective-permute-start.4 = (f32[13,16,128]{2,1,0:T(8,128)S(1)}, f32[13,16,128]{2,1,0:T(8,128)S(1)}, u32[]{:S(2)}, u32[]{:S(2)}) collective-permute-start(f32[13,16,128]{2,1,0:T(8,128)S(1)} %get-tuple-element.20.message), channel_id=1, source_target_pairs={{0,12},{4,0},{8,4},{12,8},{1,13},{5,1},{9,5},{13,9},{2,14},{6,2},{... | collective-permute-start | bytes 319496 | tf_op jit(solution)/shard_map/ppermute | solution.py:456
  22.3 3.1 %near_x.1.before = f32[4096,128]{1,0:T(8,128)S(1)} custom-call(bf16[1024,64]{1,0:T(8,128)(2,1)S(1)} %get-tuple-element.16.targets, f32[11,16,128]{2,1,0:T(8,128)S(1)} %collective-permute-done.3.outer.rest_1_.halo, f32[13,16,128]{2,1,0:T(8,128)S(1)} %get-tuple-element.20.message, f32[4096,128]{1,0:T(8,128)S(1)} %near_z.1.rest_2_.before), custom_call_target="tpu_custom_call" | custom-call | flops 6291456000 | bytes 1048576 | tf_op jit(solution)/shard_map/near_x/pallas_call | solution.py:470
  25.4 0.0 collective-permute-done.6.rest_3_
  25.4 0.0 collective-permute-done.5.low.rest_4_
  25.4 7.0 %near_y.1 = f32[3,8,128]{2,1,0:T(8,128)} custom-call(f32[3,3]{1,0:T(4,128)S(1)} %copy-done.3, f32[2,2,2]{2,1,0:T(2,128)S(1)} %copy-done.4, s32[2,2,2]{2,1,0:T(2,128)S(1)} %copy-done.1, f32[10,8,128]{2,1,0:T(8,128)S(1)} %get-tuple-element.14.own, bf16[1024,64]{1,0:T(8,128)(2,1)S(1)} %get-tuple-element.16.targets, ...), custom_call_target="tpu_custom_call" | custom-call | flops 9437184000 | bytes 1048576 | tf_op jit(solution)/shard_map/near_y/pallas_call | solution.py:470
  (10 shorter events, 0.0 us)
Async XLA Ops:
  0.8 0.7 %copy-start = (s32[2,2,2]{2,1,0:T(2,128)S(1)}, s32[2,2,2]{2,1,0:T(2,128)}, u32[]{:S(2)}) copy-start(s32[2,2,2]{2,1,0:T(2,128)} %counts.3) | copy-start | bytes 100
  2.2 11.9 %collective-permute-start.2 = (f32[8,128]{1,0:T(8,128)S(1)}, f32[8,128]{1,0:T(8,128)S(1)}, u32[]{:S(2)}, u32[]{:S(2)}) collective-permute-start(f32[8,128]{1,0:T(8,128)S(1)} %get-tuple-element.18), channel_id=1, source_target_pairs={{0,2},{1,3},{2,0},{3,1},{4,6},{5,7},{6,4},{7,5},{8,10},{9,11},{10,... | collective-permute-start | bytes 12296 | tf_op jit(solution)/shard_map/ppermute | solution.py:456
  6.3 7.8 %collective-permute-start.1 = (f32[11,4,128]{2,1,0:T(4,128)S(1)}, f32[11,4,128]{2,1,0:T(4,128)S(1)}, u32[]{:S(2)}, u32[]{:S(2)}) collective-permute-start(f32[11,4,128]{2,1,0:T(4,128)S(1)} %get-tuple-element.17), channel_id=1, source_target_pairs={{0,1},{1,2},{2,3},{3,0},{4,5},{5,6},{6,7},{7,4},{8,9},{9,10},{10,1... | collective-permute-start | bytes 67592 | tf_op jit(solution)/shard_map/ppermute | solution.py:456
  7.9 6.3 %collective-permute-start = (f32[11,4,128]{2,1,0:T(4,128)S(1)}, f32[11,4,128]{2,1,0:T(4,128)S(1)}, u32[]{:S(2)}, u32[]{:S(2)}) collective-permute-start(f32[11,4,128]{2,1,0:T(4,128)S(1)} %get-tuple-element.15.message), channel_id=1, source_target_pairs={{0,3},{1,0},{2,1},{3,2},{4,7},{5,4},{6,5},{7,6},{8,11},{9,8},{10,9... | collective-permute-start | bytes 67592 | tf_op jit(solution)/shard_map/ppermute | solution.py:456
  14.2 4.6 %collective-permute-start.3 = (f32[11,16,128]{2,1,0:T(8,128)S(1)}, f32[11,16,128]{2,1,0:T(8,128)S(1)}, u32[]{:S(2)}, u32[]{:S(2)}) collective-permute-start(f32[11,16,128]{2,1,0:T(8,128)S(1)} %pack_x.1.halo.inner.rest_0_), channel_id=1, source_target_pairs={{0,16},{16,0},{1,17},{17,1},{2,18},{18,2},{3,19},{19,3},{4,20},{20... | collective-permute-start | bytes 270344 | tf_op jit(solution)/shard_map/ppermute | solution.py:456
  18.9 6.5 %collective-permute-start.6 = (f32[4,16,128]{2,1,0:T(8,128)S(1)}, f32[4,16,128]{2,1,0:T(8,128)S(1)}, u32[]{:S(2)}, u32[]{:S(2)}) collective-permute-start(f32[4,16,128]{2,1,0:T(8,128)S(1)} %get-tuple-element.22), channel_id=1, source_target_pairs={{0,8},{4,12},{8,0},{12,4},{1,9},{5,13},{9,1},{13,5},{2,10},{6,14},... | collective-permute-start | bytes 98312 | tf_op jit(solution)/shard_map/ppermute | solution.py:456
  20.4 4.9 %collective-permute-start.5 = (f32[13,16,128]{2,1,0:T(8,128)S(1)}, f32[13,16,128]{2,1,0:T(8,128)S(1)}, u32[]{:S(2)}, u32[]{:S(2)}) collective-permute-start(f32[13,16,128]{2,1,0:T(8,128)S(1)} %get-tuple-element.21), channel_id=1, source_target_pairs={{0,4},{4,8},{8,12},{12,0},{1,5},{5,9},{9,13},{13,1},{2,6},{6,10},{... | collective-permute-start | bytes 319496 | tf_op jit(solution)/shard_map/ppermute | solution.py:456
  20.4 5.0 %copy-start.1 = (s32[2,2,2]{2,1,0:T(2,128)S(1)}, s32[2,2,2]{2,1,0:T(2,128)}, u32[]{:S(2)}) copy-start(s32[2,2,2]{2,1,0:T(2,128)} %counts.3) | copy-start | bytes 100
  20.4 5.0 %copy-start.2 = (f32[128,128]{1,0:T(8,128)S(1)}, f32[128,128]{1,0:T(8,128)}, u32[]{:S(2)}) copy-start(f32[128,128]{1,0:T(8,128)} %translation.1) | copy-start | bytes 196612
  20.4 5.0 %copy-start.3 = (f32[3,3]{1,0:T(4,128)S(1)}, f32[3,3]{1,0:T(4,128)}, u32[]{:S(2)}) copy-start(f32[3,3]{1,0:T(4,128)} %stress.1) | copy-start | bytes 112
  20.4 5.0 %copy-start.4 = (f32[2,2,2]{2,1,0:T(2,128)S(1)}, f32[2,2,2]{2,1,0:T(2,128)}, u32[]{:S(2)}) copy-start(f32[2,2,2]{2,1,0:T(2,128)} %mobility.1) | copy-start | bytes 100
  20.5 5.0 %copy-start.5 = (f32[8,256]{1,0:T(8,128)S(1)}, f32[8,256]{1,0:T(8,128)}, u32[]{:S(2)}) copy-start(f32[8,256]{1,0:T(8,128)} %constant.2.clone.weights_far) | copy-start | bytes 24580
  20.5 4.9 %collective-permute-start.4 = (f32[13,16,128]{2,1,0:T(8,128)S(1)}, f32[13,16,128]{2,1,0:T(8,128)S(1)}, u32[]{:S(2)}, u32[]{:S(2)}) collective-permute-start(f32[13,16,128]{2,1,0:T(8,128)S(1)} %get-tuple-element.20.message), channel_id=1, source_target_pairs={{0,12},{4,0},{8,4},{12,8},{1,13},{5,1},{9,5},{13,9},{2,14},{6,2},{... | collective-permute-start | bytes 319496 | tf_op jit(solution)/shard_map/ppermute | solution.py:456
